TPU v7x, 512 devices: a whole 4x4x16 slice. The times are simulated.
512 devices in a mesh: depth: 2 (over x_hi), row: 16 (over x_lo, y, core), col: 16 (over z).
Axes of the slice: x: 4 (x_hi: 2, x_lo: 2; x = x_hi * 2 + x_lo), y: 4, z: 16, core: 2. Of those that a mesh axis runs over, the one named last changes fastest.
Arguments:
- latents: bfloat16 [4096, 2432], P(('depth', 'row'), 'col'), may hold values from -6 to 6
- out_grad: bfloat16 [4096, 2432], P(('depth', 'row'), 'col'), may hold values from -2 to 2
- w_query: bfloat16 [2432, 2048], P('row', 'col'), may hold values from -0.10406108557514765 to 0.10406108557514765
- w_key: bfloat16 [2432, 2048], P('row', 'col'), may hold values from -0.10406108557514765 to 0.10406108557514765
- w_value: bfloat16 [2432, 2048], P('row', 'col'), may hold values from -0.125 to 0.125
- w_out: bfloat16 [2432, 2048], P('row', 'col'), may hold values from -1.6171875 to 1.6171875
- gain: bfloat16 [2432], P('col'), may hold values from 0.25 to 1.75
Outputs:
- latent_grad: bfloat16 [4096, 2432], P(('depth', 'row'), 'col')
All inputs are finite; a program needn't handle non-finite values.
Results may differ from a plain program's by a relative error of at most 0.024.
Values may be sent and summed in bfloat16 or wider, within the bound.
A program may use at most 64 MiB of HBM per device.

v0:
```python
import jax
import jax.numpy as jnp
from jax import lax
from jax.sharding import PartitionSpec as P

D = 2432
HDIM = 64


epsilon = 1e-06


def shards(latents, out_grad, w_query, w_key, w_value, w_out, gain):
    row_count = latents.shape[0]
    local_inner = w_query.shape[1]
    head_count = local_inner // HDIM
    x_local = latents.astype(jnp.float32)
    gain_local = gain.astype(jnp.float32)
    squares = lax.psum(jnp.sum(x_local * x_local, axis=1), "col")
    norm_scale = lax.rsqrt(squares / D + epsilon)[:, None]
    normed = lax.all_gather(
        (x_local * norm_scale * gain_local).astype(jnp.bfloat16), "col", axis=1, tiled=True
    )
    grad_full = lax.all_gather(out_grad, "col", axis=1, tiled=True)
    pieces = (
        lax.all_gather(w_query, "row", axis=0, tiled=True),
        lax.all_gather(w_key, "row", axis=0, tiled=True),
        lax.all_gather(w_value, "row", axis=0, tiled=True),
        lax.all_gather(w_out, "row", axis=0, tiled=True),
    )
    queries = jnp.dot(normed, pieces[0], preferred_element_type=jnp.float32).astype(jnp.bfloat16)
    keys_local = jnp.dot(normed, pieces[1], preferred_element_type=jnp.float32).astype(jnp.bfloat16)
    values_local = jnp.dot(normed, pieces[2], preferred_element_type=jnp.float32).astype(
        jnp.bfloat16
    )
    out_dir = jnp.dot(grad_full, pieces[3], preferred_element_type=jnp.float32).astype(jnp.bfloat16)
    query_three = queries.reshape(row_count, head_count, HDIM)
    dir_three = out_dir.reshape(row_count, head_count, HDIM)
    keys_all, values_all = (
        lax.all_gather(keys_local, "row", axis=0, tiled=True),
        lax.all_gather(values_local, "row", axis=0, tiled=True),
    )
    key_three = keys_all.reshape(-1, head_count, HDIM)
    value_three = values_all.reshape(-1, head_count, HDIM)
    query_parts = []
    key_parts = []
    value_parts = []
    for head_num in range(head_count):
        query_head = query_three[:, head_num]
        dir_head = dir_three[:, head_num]
        key_head = key_three[:, head_num]
        value_head = value_three[:, head_num]
        scores = (
            jnp.einsum("qd,kd->qk", query_head, key_head, preferred_element_type=jnp.float32)
            * 0.125
        )
        maxima = jnp.max(scores, axis=1, keepdims=True)
        expo = jnp.exp(scores - maxima)
        totals = jnp.sum(expo, axis=1, keepdims=True)
        attended = (
            jnp.dot(expo.astype(jnp.bfloat16), value_head, preferred_element_type=jnp.float32)
            / totals
        )
        probs = expo / totals
        delta = jnp.sum(dir_head.astype(jnp.float32) * attended, axis=1, keepdims=True)
        prob_grad = jnp.einsum(
            "qd,kd->qk", dir_head, value_head, preferred_element_type=jnp.float32
        )
        score_grad = (probs * (prob_grad - delta)).astype(jnp.bfloat16)
        query_parts.append(
            0.125 * jnp.dot(score_grad, key_head, preferred_element_type=jnp.float32)
        )
        key_parts.append(
            0.125
            * jnp.einsum("qk,qd->kd", score_grad, query_head, preferred_element_type=jnp.float32)
        )
        value_parts.append(
            jnp.einsum(
                "qk,qd->kd",
                probs.astype(jnp.bfloat16),
                dir_head,
                preferred_element_type=jnp.float32,
            )
        )
    query_grad = jnp.concatenate(query_parts, axis=1).astype(jnp.bfloat16)
    key_terms = jnp.concatenate(key_parts, axis=1)
    value_terms = jnp.concatenate(value_parts, axis=1)
    key_sum, value_sum = (
        lax.psum_scatter(
            key_terms.astype(jnp.bfloat16), "row", scatter_dimension=0, tiled=True
        ).astype(jnp.float32),
        lax.psum_scatter(
            value_terms.astype(jnp.bfloat16), "row", scatter_dimension=0, tiled=True
        ).astype(jnp.float32),
    )
    key_grad = key_sum.astype(jnp.bfloat16)
    value_grad = value_sum.astype(jnp.bfloat16)
    pieces = lax.all_gather((w_query, w_key, w_value), "row", axis=0, tiled=True)
    term = jnp.einsum("ti,di->td", query_grad, pieces[0], preferred_element_type=jnp.float32)
    term = term + jnp.einsum("ti,di->td", key_grad, pieces[1], preferred_element_type=jnp.float32)
    partial_grad = term + jnp.einsum(
        "ti,di->td", value_grad, pieces[2], preferred_element_type=jnp.float32
    )
    normed_grad = lax.psum_scatter(
        partial_grad.astype(jnp.bfloat16), "col", scatter_dimension=1, tiled=True
    ).astype(jnp.float32)
    scaled = normed_grad * gain_local
    local_norm = x_local * norm_scale
    inner_sum = lax.psum(jnp.sum(scaled * local_norm, axis=1), "col") / D
    raw = out_grad.astype(jnp.float32) + norm_scale * (scaled - local_norm * inner_sum[:, None])
    cell_count = raw.size * lax.axis_size("depth") * lax.axis_size("row") * lax.axis_size("col")
    grad_power = lax.psum(jnp.sum(raw * raw), ("depth", "row", "col"))
    return (raw * lax.rsqrt(grad_power / cell_count + epsilon)).astype(jnp.bfloat16)


def solution(mesh):
    return jax.shard_map(
        shards,
        mesh=mesh,
        in_specs=(
            P(("depth", "row"), "col"),
            P(("depth", "row"), "col"),
            P("row", "col"),
            P("row", "col"),
            P("row", "col"),
            P("row", "col"),
            P("col"),
        ),
        out_specs=P(("depth", "row"), "col"),
        check_vma=False,
    )
```

profile of v0, /device:TPU:1, one launch (start us, length us, event | category | flops | bytes accessed | tf_op | source)
XLA Modules:
  0.0 576.8 jit_solution(15079245587110214617)
XLA Ops:
  6.5 0.0 reduce-scatter.10.cloned.1.call-start
  6.5 0.8 fusion.33
  7.4 30.3 %psum.21 = f32[128]{0:T(128)S(1)} all-reduce(f32[128]{0:T(128)S(1)} %fusion.33), channel_id=1, replica_groups=mesh['depth'=2,'row'=16,'col'=16] {'col'}, use_global_device_ids=true, to_apply=%region_1.0 | all-reduce | flops 128 | bytes 1024 | tf_op jit(solution)/shard_map/psum | solution.py:19
  37.7 0.7 convert_element_type.66
  38.4 0.9 fusion.28
  39.2 22.8 %all_gather.27 = bf16[128,2432]{0,1:T(8,128)(2,1)S(1)} all-gather(bf16[128,152]{0,1:T(8,128)(2,1)S(1)} %fusion.28), channel_id=1, replica_groups=mesh['depth'=2,'row'=16,'col'=16] {'col'}, dimensions={1}, use_global_device_ids=true | all-gather | bytes 661504 | tf_op jit(solution)/shard_map/all_gather | solution.py:21
  62.0 36.3 %all_gather.28 = bf16[2432,128]{1,0:T(8,128)(2,1)S(1)} all-gather(bf16[152,128]{1,0:T(8,128)(2,1)} %param.9), channel_id=1, replica_groups=mesh['depth'=2,'row'=16,'col'=16] {'row'}, dimensions={0}, use_global_device_ids=true | all-gather | bytes 661504 | tf_op jit(solution)/shard_map/all_gather | solution.py:26
  98.4 0.0 copy-done.9
  98.4 18.0 %all_gather.29 = bf16[2432,128]{1,0:T(8,128)(2,1)S(1)} all-gather(bf16[152,128]{1,0:T(8,128)(2,1)S(1)} %copy-done.9), channel_id=1, replica_groups=mesh['depth'=2,'row'=16,'col'=16] {'row'}, dimensions={0}, use_global_device_ids=true | all-gather | bytes 661504 | tf_op jit(solution)/shard_map/all_gather | solution.py:27
  116.3 0.4 convolution_convert_fusion.5
  116.7 0.4 convolution_convert_fusion.4
  117.1 0.0 copy-done.2
  117.1 0.1 copy-done
  117.2 19.0 %all_gather.30 = bf16[2048,128]{1,0:T(8,128)(2,1)S(1)} all-gather(bf16[128,128]{1,0:T(8,128)(2,1)S(1)} %convolution_convert_fusion.4), channel_id=1, replica_groups=mesh['depth'=2,'row'=16,'col'=16] {'row'}, dimensions={0}, use_global_device_ids=true | all-gather | bytes 557056 | tf_op jit(solution)/shard_map/all_gather | solution.py:40
  136.2 0.2 copy.12
  136.4 0.0 copy-start.4
  136.4 0.0 copy-start.10
  136.4 0.4 fusion.41
  136.8 0.4 copy-done.4
  137.2 0.4 fusion.42
  137.6 0.0 copy-done.10
  137.6 18.0 %all_gather.33 = bf16[2432,128]{1,0:T(8,128)(2,1)S(1)} all-gather(bf16[152,128]{1,0:T(8,128)(2,1)S(1)} %copy-done.10), channel_id=1, replica_groups=mesh['depth'=2,'row'=16,'col'=16] {'row'}, dimensions={0}, use_global_device_ids=true | all-gather | bytes 661504 | tf_op jit(solution)/shard_map/all_gather | solution.py:28
  155.6 0.4 convolution_convert_fusion.2
  156.0 0.0 copy-start.8
  156.0 19.0 %all_gather.34 = bf16[2048,128]{1,0:T(8,128)(2,1)S(1)} all-gather(bf16[128,128]{1,0:T(8,128)(2,1)S(1)} %convolution_convert_fusion.2), channel_id=1, replica_groups=mesh['depth'=2,'row'=16,'col'=16] {'row'}, dimensions={0}, use_global_device_ids=true | all-gather | bytes 557056 | tf_op jit(solution)/shard_map/all_gather | solution.py:41
  175.0 1.0 copy.13
  176.0 18.0 %all_gather.32 = bf16[2432,128]{1,0:T(8,128)(2,1)S(1)} all-gather(bf16[152,128]{1,0:T(8,128)(2,1)S(1)} %copy-done.11), channel_id=1, replica_groups=mesh['depth'=2,'row'=16,'col'=16] {'row'}, dimensions={0}, use_global_device_ids=true | all-gather | bytes 661504 | tf_op jit(solution)/shard_map/all_gather | solution.py:29
  194.0 23.8 %all_gather.31 = bf16[128,2432]{0,1:T(8,128)(2,1)S(1)} all-gather(bf16[128,152]{0,1:T(8,128)(2,1)S(1)} %copy-done.8), channel_id=1, replica_groups=mesh['depth'=2,'row'=16,'col'=16] {'col'}, dimensions={1}, use_global_device_ids=true | all-gather | bytes 661504 | tf_op jit(solution)/shard_map/all_gather | solution.py:24
  217.8 0.4 convolution_convert_fusion.3
  218.2 0.3 fusion.18
  218.5 0.4 copy-done.6
  218.9 0.4 fusion.12
  219.3 0.4 fusion.4
  219.6 0.2 fusion.6
  219.9 0.3 fusion.15
  220.1 0.4 fusion.11
  220.5 1.2 fusion.3
  221.7 1.3 fusion.5
  223.0 0.9 pad_maximum_fusion
  223.9 2.1 copy.14
  225.9 0.0 reduce-scatter.10.cloned.1.call-update
  225.9 0.0 reduce-scatter.12.cloned.1.call-start
  226.0 0.4 convolution_convert_fusion
  226.4 0.4 convolution_convert_fusion.1
  226.8 0.0 copy-start.5
  226.8 1.0 copy.16
  227.9 0.0 reduce-scatter.12.cloned.1.call-update
  227.9 0.0 reduce-scatter.14.cloned.1.call-start
  228.0 0.3 fusion.10
  228.3 1.4 fusion.9
  229.7 1.3 fusion.34
  231.0 61.6 %reduce-scatter.10.cloned.1.call-done = bf16[128,128]{1,0:T(8,128)(2,1)} async-done(((bf16[2048,128]{1,0:T(8,128)(2,1)}), bf16[128,128]{1,0:T(8,128)(2,1)}) %reduce-scatter.10.cloned.1.call-update) | async-done | bytes 32784
  292.7 1.6 convolution_add_fusion.1
  294.3 0.0 copy-start.7
  294.3 68.2 %reduce-scatter.12.cloned.1.call-done = bf16[128,128]{1,0:T(8,128)(2,1)} async-done(((bf16[2048,128]{1,0:T(8,128)(2,1)}), bf16[128,128]{1,0:T(8,128)(2,1)}) %reduce-scatter.12.cloned.1.call-update) | async-done | bytes 32784
  362.6 1.9 fusion
  364.4 0.0 reduce-scatter.14.cloned.1.call-update
  364.5 60.3 %reduce-scatter.14.cloned.1.call-done = bf16[128,152]{0,1:T(8,128)(2,1)} async-done(((bf16[128,2432]{0,1:T(8,128)(2,1)}), bf16[128,152]{0,1:T(8,128)(2,1)}) %reduce-scatter.14.cloned.1.call-update) | async-done | bytes 38928
  424.8 0.0 copy-done.7
  424.8 0.9 fusion.29
  425.7 22.1 %psum.22 = f32[128]{0:T(128)S(1)} all-reduce(f32[128]{0:T(128)S(1)} %fusion.29), channel_id=1, replica_groups=mesh['depth'=2,'row'=16,'col'=16] {'col'}, use_global_device_ids=true, to_apply=%region_12.0 | all-reduce | flops 128 | bytes 1024 | tf_op jit(solution)/shard_map/psum | solution.py:109
  447.7 1.5 multiply_reduce_fusion
  449.2 118.9 %psum.23 = f32[]{:T(128)} all-reduce(f32[]{:T(128)} %multiply_reduce_fusion), channel_id=1, replica_groups=mesh['depth'=2,'row'=16,'col'=16] {'depth','row','col'}, use_global_device_ids=true, to_apply=%region_14.0 | all-reduce | flops 1 | bytes 8 | tf_op jit(solution)/shard_map/psum | solution.py:112
  568.8 1.5 multiply_convert_fusion
  (15 shorter events, 0.1 us)
Async XLA Ops:
  6.5 91.8 %copy-start.9 = (bf16[152,128]{1,0:T(8,128)(2,1)S(1)}, bf16[152,128]{1,0:T(8,128)(2,1)}, u32[]{:S(2)}) copy-start(bf16[152,128]{1,0:T(8,128)(2,1)} %param.10) | copy-start | bytes 116740
  6.5 286.1 %reduce-scatter.10.cloned.1.call-start = ((), (), s32[]{:S(2)}) async-start(), calls=%async_computation.3 | async-start | bytes 557056
  98.4 18.7 %copy-start.2 = (bf16[2432,128]{1,0:T(8,128)(2,1)}, bf16[2432,128]{1,0:T(8,128)(2,1)S(1)}, u32[]{:S(2)}) copy-start(bf16[2432,128]{1,0:T(8,128)(2,1)S(1)} %all_gather.28) | copy-start | bytes 1867780
  116.3 0.9 copy-start
  136.4 0.8 copy-start.4
  136.4 1.2 copy-start.10
  155.6 20.4 %copy-start.11 = (bf16[152,128]{1,0:T(8,128)(2,1)S(1)}, bf16[152,128]{1,0:T(8,128)(2,1)}, u32[]{:S(2)}) copy-start(bf16[152,128]{1,0:T(8,128)(2,1)} %param.12) | copy-start | bytes 116740
  156.0 38.0 %copy-start.8 = (bf16[128,152]{0,1:T(8,128)(2,1)S(1)}, bf16[128,152]{0,1:T(8,128)(2,1)}, u32[]{:S(2)}) copy-start(bf16[128,152]{0,1:T(8,128)(2,1)} %param.8) | copy-start | bytes 116740
  217.8 1.0 copy-start.6
  225.9 136.6 %reduce-scatter.12.cloned.1.call-start = ((), (), s32[]{:S(2)}) async-start(), calls=%async_computation.4 | async-start | bytes 557056
  226.8 1.2 copy-start.5
  227.9 1.8 copy-start.3
  227.9 196.9 %reduce-scatter.14.cloned.1.call-start = ((), (), s32[]{:S(2)}) async-start(), calls=%async_computation.5 | async-start | bytes 661504
  228.3 64.4 %copy-start.1 = (bf16[2432,128]{1,0:T(8,128)(2,1)S(1)}, bf16[2432,128]{1,0:T(8,128)(2,1)}, u32[]{:S(2)}) copy-start(bf16[2432,128]{1,0:T(8,128)(2,1)} %copy-done) | copy-start | bytes 1867780
  294.3 130.5 %copy-start.7 = (bf16[128,152]{0,1:T(8,128)(2,1)S(1)}, bf16[128,152]{0,1:T(8,128)(2,1)}, u32[]{:S(2)}) copy-start(bf16[128,152]{0,1:T(8,128)(2,1)} %param.7) | copy-start | bytes 116740
Sparse Core Ops, SparseCore 0:
  226.1 66.5 reduce-scatter.9
  295.7 66.8 reduce-scatter.11
  365.4 59.3 reduce-scatter.13
where the time goes:
time: 578 us; the launch traced here: 577 us
  blocking collectives  346 us (60%)
  waiting for transfers between devices  190 us (33%)
  between operations  14 us (2%)
  matrix products  13.5 us (2%)
  other arithmetic  7.68 us (1%)
    unnamed x6, waiting for transfers between devices  190 us
    psum x1, blocking collectives, shards(): grad_power = lax.psum(jnp.sum(raw * raw), ('depth', 'row', 'col'))  119 us
    all_gather x1, blocking collectives, shards(): lax.all_gather(w_query, 'row', axis=0, tiled=True)  36.3 us
    psum x1, blocking collectives, shards(): squares = lax.psum(jnp.sum(x_local * x_local, axis=1), 'col')  30.3 us
    all_gather x1, blocking collectives, shards(): grad_full = lax.all_gather(out_grad, 'col', axis=1, tiled=True)  23.8 us
    all_gather x1, blocking collectives, shards(): lax.all_gather((x_local * norm_scale * gain_local).astype(jnp.bfloat16),...  22.8 us
    psum x1, blocking collectives, shards(): inner_sum = lax.psum(jnp.sum(scaled * local_norm, axis=1), 'col') / D  22.1 us
    all_gather x1, blocking collectives, shards(): lax.all_gather(values_local, 'row', axis=0, tiled=True)  19 us
  transfers between devices with their start and end apart: 3, of which 3 were waited for; matrix products, arithmetic and copies ran while one was open for 1% of the time, Pallas kernels for 0%

commit v1 on v0

v1 whole, which is shorter than its diff:
```python
import functools

import jax
import jax.numpy as jnp
from jax import lax
from jax.experimental import pallas as pl
from jax.experimental.pallas import tpu as pltpu
from jax.sharding import PartitionSpec as P

MESH = pl.DeviceIdType.MESH
F32 = jnp.float32
BF16 = jnp.bfloat16
FEAT = 152
PAD = 160
HALF = 80
TOK = 128
WIDE = 128
HDIM = 64
SLOT = 256
epsilon = 1e-06


def dot_nt(a, b):
    return lax.dot_general(a, b, (((1,), (1,)), ((), ())), preferred_element_type=F32)


def dot_tn(a, b):
    return lax.dot_general(a, b, (((0,), (0,)), ((), ())), preferred_element_type=F32)


def dot_nn(a, b):
    return jnp.dot(a, b, preferred_element_type=F32)


def eye(rows, columns):
    at = lax.broadcasted_iota(jnp.int32, (rows, columns), 0)
    to = lax.broadcasted_iota(jnp.int32, (rows, columns), 1)
    return jnp.where(at == to, 1.0, 0.0).astype(BF16)


def kernel(
    sizes,
    lat_ref, og_ref, wq_ref, wk_ref, wv_ref, wo_ref, gain_ref,
    out_ref,
    xt_all, og_all, wkv_all, wqo_all, kv_all,
    xt_own, og_own, gain_own,
    s_ref, dp_ref, terms, sib_rx, pair_sum, rx,
    rs_tx, rs_right, rs_left,
    pw_tx, pw0, pw1, pw2,
    z_send, z_recv,
    w_send, w_recv, wsib_send, wsib_recv,
    kv_send, kv_recv, kvsib_send, kvsib_recv,
    t_send, t_recv, r_send, r_recv,
    rs_send, rs_recv,
    p_send, p_recv,
):
    depths, los, ys, zs = sizes
    xs = depths * los
    chips = los * ys
    planes = xs * ys
    rows = chips * 2
    seq = rows * TOK
    right_steps = zs // 2
    left_steps = zs - 1 - right_steps

    d = lax.axis_index("depth")
    r = lax.axis_index("row")
    c = lax.axis_index("col")
    core = lax.rem(r, 2)
    other = 1 - core
    chip = r // 2
    lo = chip // ys
    y = lax.rem(chip, ys)
    x = d * los + lo
    here = x * ys + y

    sibling = (d, chip * 2 + other, c)
    z_right = (d, r, lax.rem(c + 1, zs))
    z_left = (d, r, lax.rem(c + zs - 1, zs))

    def plane_device(at):
        to_x, to_y = at // ys, lax.rem(at, ys)
        return (to_x // los, (lax.rem(to_x, los) * ys + to_y) * 2 + core, c)

    def chip_device(to_chip):
        return (d, to_chip * 2 + core, c)

    def remote(src, dst, send, recv, device):
        return pltpu.make_async_remote_copy(
            src_ref=src, dst_ref=dst, send_sem=send, recv_sem=recv, device_id=device, device_id_type=MESH
        )

    barrier = pltpu.get_barrier_semaphore()

    def greet(device):
        pl.semaphore_signal(barrier, inc=1, device_id=device, device_id_type=MESH)

    greet(sibling)

    @pl.loop(1, zs)
    def _(i):
        greet((d, r, lax.rem(c + i, zs)))

    @pl.loop(1, planes)
    def _(i):
        greet(plane_device(lax.rem(here + i, planes)))

    row_at = lax.broadcasted_iota(jnp.int32, (PAD, TOK), 0)
    turn = eye(PAD, FEAT)
    xt = dot_nt(turn, lat_ref[...])
    ogt = dot_nt(turn, og_ref[...])
    gain_diag = turn * gain_ref[...]
    gain_wide = dot_nt(gain_diag, jnp.ones((TOK, FEAT), BF16))
    squares = jnp.sum(xt * xt, axis=0, keepdims=True)
    square_hi = squares.astype(BF16).astype(F32)
    rest = squares - square_hi
    square_mid = rest.astype(BF16).astype(F32)
    square_lo = rest - square_mid
    sent = xt * gain_wide
    sent = jnp.where(row_at == FEAT, square_hi, sent)
    sent = jnp.where(row_at == FEAT + 1, square_mid, sent)
    sent = jnp.where(row_at == FEAT + 2, square_lo, sent)
    xt_all[c] = sent.astype(BF16)
    og_all[c] = ogt.astype(BF16)
    xt_own[...] = xt
    og_own[...] = ogt
    gain_own[...] = gain_wide
    nothing = jnp.zeros((PAD - FEAT, WIDE), BF16)

    def padded(w_ref):
        return jnp.concatenate([w_ref[...], nothing], axis=0)

    wkv_all[r] = jnp.concatenate([padded(wk_ref), padded(wv_ref)], axis=1)
    wqo_all[r] = jnp.concatenate([padded(wq_ref), padded(wo_ref)], axis=1)

    pl.semaphore_wait(barrier, 1 + (zs - 1) + (planes - 1))

    gathers = (xt_all, og_all)

    def ring_right(array, step):
        slot = gathers[array].at[lax.rem(c + zs - step, zs)]
        return remote(slot, slot, z_send.at[array, 0, step], z_recv.at[array, 0, step], z_right)

    def ring_right_came(array, step):
        slot = gathers[array].at[lax.rem(c + 2 * zs - 1 - step, zs)]
        remote(slot, slot, z_send.at[array, 0, step], z_recv.at[array, 0, step], z_right).wait_recv()

    def ring_left(array, step):
        slot = gathers[array].at[lax.rem(c + step, zs)]
        return remote(slot, slot, z_send.at[array, 1, step], z_recv.at[array, 1, step], z_left)

    def ring_left_came(array, step):
        slot = gathers[array].at[lax.rem(c + 1 + step, zs)]
        remote(slot, slot, z_send.at[array, 1, step], z_recv.at[array, 1, step], z_left).wait_recv()

    weights = (wkv_all, wqo_all)

    def weight_column(array, i):
        slot = weights[array].at[r]
        to = x * ys + lax.rem(y + i, ys)
        return remote(slot, slot, w_send.at[array, i], w_recv.at[array, chip], plane_device(to))

    def weight_across(array, i, side):
        slot = weights[array].at[r, pl.ds(side * HALF, HALF)]
        to = lax.rem(x + (1 if side == 0 else xs - 1), xs) * ys + lax.rem(y + i, ys)
        return remote(
            slot, slot, w_send.at[array, ys * (1 + side) + i], w_recv.at[array, chip], plane_device(to)
        )

    def weight_sibling(array, of_chip):
        slot = weights[array].at[of_chip * 2 + core]
        return remote(slot, slot, wsib_send.at[array, of_chip], wsib_recv.at[array, of_chip], sibling)

    def weight_sibling_came(array, of_chip):
        slot = weights[array].at[of_chip * 2 + other]
        remote(slot, slot, wsib_send.at[array, of_chip], wsib_recv.at[array, of_chip], sibling).wait_recv()

    def weight_came(array, of_chip):
        slot = weights[array].at[of_chip * 2 + core]
        remote(slot, slot, w_send.at[array, 0], w_recv.at[array, of_chip], sibling).wait_recv()

    def weight_start(array):
        weight_sibling(array, chip).start()

        @pl.loop(1, ys)
        def _(i):
            weight_column(array, i).start()

        if los > 1:

            @pl.loop(0, ys)
            def _(i):
                weight_across(array, i, 0).start()
                weight_across(array, i, 1).start()

    def nth_chip(t):
        same = t < ys - 1
        of_lo = jnp.where(same, lo, los - 1 - lo)
        of_y = lax.rem(y + jnp.where(same, 1 + t, t - (ys - 1)), ys)
        return of_lo * ys + of_y

    for array in range(2):
        ring_right(array, 0).start()
        ring_left(array, 0).start()
    weight_start(0)
    weight_start(1)

    @pl.loop(1, right_steps)
    def _(step):
        for array in range(2):
            ring_right_came(array, step - 1)
            ring_right(array, step).start()
            ring_left_came(array, step - 1)

            @pl.when(step < left_steps)
            def _():
                ring_left(array, step).start()

        of_chip = nth_chip(step - 1)
        weight_came(0, of_chip)
        weight_sibling(0, of_chip).start()

    ring_right_came(0, right_steps - 1)

    @pl.loop(0, chips)
    def _(i):
        weight_sibling_came(0, i)

    tails = jnp.zeros((16, TOK), F32)
    for j in range(zs):
        tails = tails + xt_all[j, PAD - 16 : PAD, :].astype(F32)
    square_sum = jnp.sum(tails[8:16], axis=0, keepdims=True)
    scale_row = lax.rsqrt(square_sum * (1.0 / (zs * FEAT)) + epsilon)
    scale_wide = jnp.transpose(jnp.broadcast_to(scale_row, (TOK, TOK)))
    scale_two = jnp.concatenate([scale_wide, scale_wide], axis=1)
    group = 4

    def project(source, weight, lanes):
        def body(i, total):
            a = source[pl.ds(i * group, group)].reshape(group * PAD, TOK)
            b = weight[pl.ds(i * group, group), :, lanes]
            return total + dot_tn(a, b.reshape(group * PAD, b.shape[-1]))

        width = lanes.stop - lanes.start
        return lax.fori_loop(0, zs // group, body, jnp.zeros((TOK, width), F32))

    kv = (project(xt_all, wkv_all, slice(0, SLOT)) * scale_two).astype(BF16)
    kv_all[r] = kv

    def kv_copy(i):
        slot = kv_all.at[r]
        return remote(
            slot, slot, kv_send.at[i], kv_recv.at[chip], chip_device(lax.rem(chip + i, chips))
        )

    def kv_came(of_chip):
        slot = kv_all.at[of_chip * 2 + core]
        remote(slot, slot, kv_send.at[0], kv_recv.at[of_chip], sibling).wait_recv()

    def kv_sibling(of_chip):
        slot = kv_all.at[of_chip * 2 + core]
        return remote(slot, slot, kvsib_send.at[of_chip], kvsib_recv.at[of_chip], sibling)

    def kv_sibling_came(of_chip):
        slot = kv_all.at[of_chip * 2 + other]
        remote(slot, slot, kvsib_send.at[of_chip], kvsib_recv.at[of_chip], sibling).wait_recv()

    @pl.loop(1, chips)
    def _(i):
        kv_copy(i).start()

    kv_sibling(chip).start()

    @pl.loop(0, chips - 1)
    def _(t):
        of_chip = nth_chip(t)
        weight_came(1, of_chip)
        weight_sibling(1, of_chip).start()

    ring_right_came(1, right_steps - 1)

    @pl.loop(0, chips)
    def _(i):
        weight_sibling_came(1, i)

    queries = (project(xt_all, wqo_all, slice(0, WIDE)) * scale_wide).astype(BF16)
    out_dir = project(og_all, wqo_all, slice(WIDE, SLOT)).astype(BF16)
    low = lax.broadcasted_iota(jnp.int32, (TOK, WIDE), 1) < HDIM

    def stacked(a):
        wide = a.astype(F32)
        parts = [jnp.where(low, wide, 0.0), jnp.where(low, 0.0, wide)]
        return jnp.concatenate(parts, axis=0).astype(BF16)

    query_stack = stacked(queries.astype(F32) * 0.125)
    dir_stack = stacked(out_dir)

    @pl.loop(1, chips)
    def _(i):
        of_chip = lax.rem(chip + chips - i, chips)
        kv_came(of_chip)
        kv_sibling(of_chip).start()

    @pl.loop(0, chips)
    def _(i):
        kv_sibling_came(i)

    block = 2 * TOK

    def keys_of(i):
        return kv_all[pl.ds(i * 2, 2), :, 0:WIDE].reshape(block, WIDE)

    def values_of(i):
        return kv_all[pl.ds(i * 2, 2), :, WIDE:SLOT].reshape(block, WIDE)

    def folded(a):
        return a.reshape(block // 8, 8, SLOT)

    def scores_body(i, most):
        scores = dot_nt(keys_of(i), query_stack)
        s_ref[i] = scores
        return jnp.maximum(most, jnp.max(folded(scores), axis=0))

    most = lax.fori_loop(0, chips, scores_body, jnp.full((8, SLOT), -jnp.inf, F32))
    most = jnp.max(most, axis=0, keepdims=True)

    def expo_body(i, sums):
        expo = jnp.exp(s_ref[i] - most)
        s_ref[i] = expo
        prob_grad = dot_nt(values_of(i), dir_stack)
        dp_ref[i] = prob_grad
        return sums[0] + jnp.sum(folded(expo), axis=0), sums[1] + jnp.sum(folded(expo * prob_grad), axis=0)

    zero = jnp.zeros((8, SLOT), F32)
    totals, delta = lax.fori_loop(0, chips, expo_body, (zero, zero))
    inverse = 1.0 / jnp.sum(totals, axis=0, keepdims=True)
    delta = jnp.sum(delta, axis=0, keepdims=True) * inverse

    def term_sibling(of_chip):
        return remote(
            terms.at[of_chip * 2 + other], sib_rx.at[of_chip], t_send.at[of_chip], t_recv.at[of_chip], sibling
        )

    def term_copy(of_chip):
        return remote(
            pair_sum.at[of_chip], rx.at[chip], r_send.at[of_chip], r_recv.at[chip], chip_device(of_chip)
        )

    def term_came(of_chip):
        remote(
            pair_sum.at[of_chip], rx.at[of_chip], r_send.at[of_chip], r_recv.at[of_chip], sibling
        ).wait_recv()

    def pair(of_chip):
        term_sibling(of_chip).wait_recv()
        own = terms[of_chip * 2 + core].astype(F32)
        pair_sum[of_chip] = (own + sib_rx[of_chip].astype(F32)).astype(BF16)

    def grads_body(n, query_grad):
        i = lax.rem(chip + 1 + n, chips)
        probs = s_ref[i] * inverse
        score_grad = (probs * (dp_ref[i] - delta)).astype(BF16)
        key_term = dot_nn(score_grad, query_stack)
        value_term = dot_nn(probs.astype(BF16), dir_stack)
        both = jnp.concatenate([key_term, value_term], axis=1).astype(BF16)
        terms[pl.ds(i * 2, 2)] = both.reshape(2, TOK, SLOT)
        term_sibling(i).start()

        @pl.when(n > 0)
        def _():
            before = lax.rem(chip + n, chips)
            pair(before)
            term_copy(before).start()

        return query_grad + dot_tn(keys_of(i), score_grad)

    query_grad = lax.fori_loop(0, chips, grads_body, jnp.zeros((WIDE, SLOT), F32))
    query_grad = jnp.concatenate([query_grad[0:HDIM, 0:TOK], query_grad[HDIM:WIDE, TOK:SLOT]], axis=0)
    query_grad = (query_grad * 0.125).astype(BF16)
    pair(chip)
    total = pair_sum[chip].astype(F32)

    def sum_body(i, total):
        of_chip = lax.rem(chip + chips - i, chips)
        term_came(of_chip)
        return total + rx[of_chip].astype(F32)

    kv_grad = lax.fori_loop(1, chips, sum_body, total).astype(BF16)

    queries_turned = dot_nt(eye(WIDE, WIDE), queries)
    inner = jnp.sum(query_grad.astype(F32) * queries_turned, axis=0, keepdims=True)
    kv_inner = kv_grad.astype(F32) * kv.astype(F32)
    kv_hi = kv_inner.astype(BF16)
    kv_lo = (kv_inner - kv_hi.astype(F32)).astype(BF16)
    ones = jnp.ones((8, SLOT), BF16)
    kv_inner = dot_nt(ones, kv_hi) + dot_nt(ones, kv_lo)
    inner = inner + kv_inner[0:1]

    def partial(j):
        value = dot_nt(wkv_all[j], kv_grad) + dot_nn(wqo_all[j, :, 0:WIDE], query_grad)
        return jnp.where(row_at == FEAT, inner, value)

    def rs_copy(src, side, step):
        dst = (rs_right, rs_left)[side].at[step]
        return remote(src, dst, rs_send.at[side, step], rs_recv.at[side, step], (z_right, z_left)[side])

    def rs_came(side, step):
        rs_copy(rs_tx.at[side], side, step).wait_recv()

    rs_tx[0] = partial(lax.rem(c + right_steps, zs)).astype(BF16)
    rs_copy(rs_tx.at[0], 0, 0).start()
    rs_tx[1] = partial(lax.rem(c + zs - left_steps, zs)).astype(BF16)
    rs_copy(rs_tx.at[1], 1, 0).start()

    @pl.loop(1, right_steps)
    def _(step):
        to_right = partial(lax.rem(c + right_steps - step, zs))
        to_left = partial(lax.rem(c + zs - left_steps + step, zs))
        rs_came(0, step - 1)
        rs_right[step - 1] = (rs_right[step - 1].astype(F32) + to_right).astype(BF16)
        rs_copy(rs_right.at[step - 1], 0, step).start()
        rs_came(1, step - 1)

        @pl.when(step < left_steps)
        def _():
            rs_left[step - 1] = (rs_left[step - 1].astype(F32) + to_left).astype(BF16)
            rs_copy(rs_left.at[step - 1], 1, step).start()

    own = partial(c) + rs_left[left_steps - 1].astype(F32)
    rs_came(0, right_steps - 1)
    own = own + rs_right[right_steps - 1].astype(F32)

    inner = own[FEAT : FEAT + 1] * (1.0 / (zs * FEAT))
    scaled = own * gain_own[...]
    normalized = xt_own[...] * scale_row
    raw = og_own[...] + scale_row * (scaled - normalized * inner)
    power = jnp.sum((raw * raw).reshape(PAD // 8, 8, TOK), axis=0)

    def power_sibling():
        return remote(pw_tx.at[0], pw0, p_send.at[0, 0], p_recv.at[0, 0], sibling)

    def power_plane(i):
        to = plane_device(lax.rem(here + i, planes))
        return remote(pw_tx.at[1], pw1.at[here], p_send.at[1, i], p_recv.at[1, here], to)

    def power_plane_came(i):
        of = lax.rem(here + i, planes)
        remote(pw_tx.at[1], pw1.at[of], p_send.at[1, i], p_recv.at[1, of], sibling).wait_recv()

    def power_col(i):
        return remote(pw_tx.at[2], pw2.at[c], p_send.at[2, i], p_recv.at[2, c], (d, r, lax.rem(c + i, zs)))

    def power_col_came(i):
        of = lax.rem(c + i, zs)
        remote(pw_tx.at[2], pw2.at[of], p_send.at[2, i], p_recv.at[2, of], sibling).wait_recv()

    pw_tx[0] = power
    power_sibling().start()
    power_sibling().wait_recv()
    power = power + pw0[...]
    pw_tx[1] = power
    pw1[here] = power

    @pl.loop(1, planes)
    def _(i):
        power_plane(i).start()

    @pl.loop(1, planes)
    def _(i):
        power_plane_came(i)

    power = jnp.sum(pw1[...], axis=0)
    pw_tx[2] = power
    pw2[c] = power

    @pl.loop(1, zs)
    def _(i):
        power_col(i).start()

    @pl.loop(1, zs)
    def _(i):
        power_col_came(i)

    power = jnp.sum(jnp.sum(pw2[...], axis=0), axis=0, keepdims=True)
    power = jnp.sum(power, axis=1, keepdims=True)
    cells = depths * seq * zs * FEAT
    final = (raw * lax.rsqrt(power * (1.0 / cells) + epsilon)).astype(BF16)
    out_ref[...] = dot_nt(eye(TOK, TOK), final)[:, 0:FEAT].astype(BF16)

    for array in range(2):

        @pl.loop(0, right_steps)
        def _(step):
            ring_right(array, step).wait_send()

        @pl.loop(0, left_steps)
        def _(step):
            ring_left(array, step).wait_send()

        @pl.loop(1, ys)
        def _(i):
            weight_column(array, i).wait_send()

        if los > 1:

            @pl.loop(0, ys)
            def _(i):
                weight_across(array, i, 0).wait_send()
                weight_across(array, i, 1).wait_send()

        @pl.loop(0, chips)
        def _(i):
            weight_sibling(array, i).wait_send()

    @pl.loop(1, chips)
    def _(i):
        kv_copy(i).wait_send()
        term_copy(lax.rem(chip + i, chips)).wait_send()

    @pl.loop(0, chips)
    def _(i):
        kv_sibling(i).wait_send()
        term_sibling(i).wait_send()

    @pl.loop(0, right_steps)
    def _(step):
        rs_copy(rs_tx.at[0], 0, step).wait_send()

    @pl.loop(0, left_steps)
    def _(step):
        rs_copy(rs_tx.at[1], 1, step).wait_send()

    power_sibling().wait_send()

    @pl.loop(1, planes)
    def _(i):
        power_plane(i).wait_send()

    @pl.loop(1, zs)
    def _(i):
        power_col(i).wait_send()


def sizes_of(mesh):
    depths, rows, zs = mesh.shape["depth"], mesh.shape["row"], mesh.shape["col"]
    los = 2
    return depths, los, rows // (2 * los), zs


def solution(mesh):
    depths, los, ys, zs = sizes_of(mesh)
    chips, planes = los * ys, depths * los * ys
    rows = chips * 2
    right_steps = zs // 2
    left_steps = zs - 1 - right_steps
    dma = pltpu.SemaphoreType.DMA
    scratch = [
        pltpu.VMEM((zs, PAD, TOK), BF16),
        pltpu.VMEM((zs, PAD, TOK), BF16),
        pltpu.VMEM((rows, PAD, SLOT), BF16),
        pltpu.VMEM((rows, PAD, SLOT), BF16),
        pltpu.VMEM((rows, TOK, SLOT), BF16),
        pltpu.VMEM((PAD, TOK), F32),
        pltpu.VMEM((PAD, TOK), F32),
        pltpu.VMEM((PAD, TOK), F32),
        pltpu.VMEM((chips, 2 * TOK, SLOT), F32),
        pltpu.VMEM((chips, 2 * TOK, SLOT), F32),
        pltpu.VMEM((rows, TOK, SLOT), BF16),
        pltpu.VMEM((chips, TOK, SLOT), BF16),
        pltpu.VMEM((chips, TOK, SLOT), BF16),
        pltpu.VMEM((chips, TOK, SLOT), BF16),
        pltpu.VMEM((2, PAD, TOK), BF16),
        pltpu.VMEM((right_steps, PAD, TOK), BF16),
        pltpu.VMEM((left_steps, PAD, TOK), BF16),
        pltpu.VMEM((3, 8, TOK), F32),
        pltpu.VMEM((8, TOK), F32),
        pltpu.VMEM((planes, 8, TOK), F32),
        pltpu.VMEM((zs, 8, TOK), F32),
        dma((2, 2, right_steps)), dma((2, 2, right_steps)),
        dma((2, 3 * ys)), dma((2, chips)), dma((2, chips)), dma((2, chips)),
        dma((chips,)), dma((chips,)), dma((chips,)), dma((chips,)),
        dma((chips,)), dma((chips,)), dma((chips,)), dma((chips,)),
        dma((2, right_steps)), dma((2, right_steps)),
        dma((3, max(planes, zs))), dma((3, max(planes, zs))),
    ]

    def shards(latents, out_grad, w_query, w_key, w_value, w_out, gain):
        vmem = pl.BlockSpec(memory_space=pltpu.VMEM)
        return pl.pallas_call(
            functools.partial(kernel, (depths, los, ys, zs)),
            out_shape=jax.ShapeDtypeStruct((TOK, FEAT), BF16),
            in_specs=[vmem] * 7,
            out_specs=vmem,
            scratch_shapes=scratch,
            compiler_params=pltpu.CompilerParams(
                collective_id=0, has_side_effects=True, vmem_limit_bytes=40 * 1024 * 1024
            ),
        )(latents, out_grad, w_query, w_key, w_value, w_out, gain.reshape(1, FEAT))

    return jax.shard_map(
        shards,
        mesh=mesh,
        in_specs=(
            P(("depth", "row"), "col"),
            P(("depth", "row"), "col"),
            P("row", "col"),
            P("row", "col"),
            P("row", "col"),
            P("row", "col"),
            P("col"),
        ),
        out_specs=P(("depth", "row"), "col"),
        check_vma=False,
    )
```

time: 578 us -> 122 us (0.21)
  blocking collectives: 346 us -> 0 us
  waiting for transfers between devices: 190 us -> 0 us
  Pallas kernels: 0 us -> 118 us
  between operations: 14 us -> 0.07 us
  matrix products: 13.5 us -> 0 us
  other arithmetic: 7.68 us -> 0 us
    unnamed x6 -> x0, waiting for transfers between devices: 190 us -> none
    all_gather x8 -> x0, blocking collectives: 175 us -> none  [the longest x1 36.3 us: shards(): lax.all_gather(w_query, 'row', axis=0, tiled=True)]
    psum x3 -> x0, blocking collectives: 171 us -> none  [the longest x1 119 us: shards(): grad_power = lax.psum(jnp.sum(raw * raw), ('depth', 'row', 'col'))]
    pallas_call x0 -> x1, Pallas kernels: none -> 118 us  [shards(): pl.pallas_call(functools.partial(kernel, (depths, los, ys, zs)), out_shap...]
    dot_general x19 -> x0, matrix products: 13.5 us -> none  [the longest x1 1.9 us: shards(): jnp.einsum('ti,di->td', value_grad, pieces[2], preferred_element_type=jnp...]
  transfers between devices with their start and end apart: 3 -> 0, of which waited for: 3 -> 0; matrix products, arithmetic and copies ran while one was open for 1% -> 0% of each run, Pallas kernels for 0% -> 0%
where the time goes in v1:
time: 122 us; the launch traced here: 121 us
  Pallas kernels  118 us (97%)
  local copies, waits for them, and re-layouts  3.02 us (2%)
    pallas_call x1, Pallas kernels, shards(): pl.pallas_call(functools.partial(kernel, (depths, los, ys, zs)), out_shap...  118 us

profile of v1, /device:TPU:1, one launch (start us, length us, event | category | flops | bytes accessed | tf_op | source)
XLA Modules:
  0.0 121.3 jit_solution(3916851223525463642)
XLA Ops:
  0.0 0.0 copy-start.4
  0.0 0.7 reshape.3.gain_ref
  0.7 0.0 copy-start.2
  0.7 0.0 copy-start.3
  0.7 0.9 copy.8.lat_ref
  1.6 0.0 copy-done.4
  1.6 0.0 copy-start
  1.6 0.0 copy-start.1
  1.6 0.1 copy.9.og_ref
  1.7 0.0 copy-done.2
  1.7 0.0 copy-done.3
  1.7 0.6 copy-done
  2.3 0.0 copy-done.1
  2.4 118.2 %shard_map.73 = bf16[128,152]{1,0:T(8,128)(2,1)S(1)} custom-call(bf16[128,152]{1,0:T(8,128)(2,1)S(1)} %copy.8.lat_ref, bf16[128,152]{1,0:T(8,128)(2,1)S(1)} %copy.9.og_ref, bf16[152,128]{1,0:T(8,128)(2,1)S(1)} %copy-done, bf16[152,128]{1,0:T(8,128)(2,1)S(1)} %copy-done.1, bf16[152,128]{1,0:T(8,128)(2,1)S(1)} %copy-done.2, bf16[152,128]{1,0:T(8,128)(2,1)S(1)} %copy-done.3, ...), custom_call_target="tpu_custom_call" | custom-call | tf_op jit(solution)/shard_map/pallas_call | solution.py:589
  120.6 0.7 copy.10
Async XLA Ops:
  0.0 1.6 %copy-start.4 = (bf16[128,152]{0,1:T(8,128)(2,1)S(1)}, bf16[128,152]{0,1:T(8,128)(2,1)}, u32[]{:S(2)}) copy-start(bf16[128,152]{0,1:T(8,128)(2,1)} %param.8) | copy-start | bytes 116740
  0.7 1.0 copy-start.2
  0.7 1.0 copy-start.3
  1.6 0.8 copy-start
  1.6 0.8 copy-start.1

commit v2 on v0

v2 whole, which is shorter than its diff:
```python
import functools

import jax
import jax.numpy as jnp
from jax import lax
from jax.experimental import pallas as pl
from jax.experimental.pallas import tpu as pltpu
from jax.sharding import PartitionSpec as P

MESH = pl.DeviceIdType.MESH
F32 = jnp.float32
BF16 = jnp.bfloat16
FEAT = 152
PAD = 160
HALF = 80
TOK = 128
WIDE = 128
HDIM = 64
SLOT = 256
epsilon = 1e-06


def dot_nt(a, b):
    return lax.dot_general(a, b, (((1,), (1,)), ((), ())), preferred_element_type=F32)


def dot_tn(a, b):
    return lax.dot_general(a, b, (((0,), (0,)), ((), ())), preferred_element_type=F32)


def dot_nn(a, b):
    return jnp.dot(a, b, preferred_element_type=F32)


def eye(rows, columns):
    at = lax.broadcasted_iota(jnp.int32, (rows, columns), 0)
    to = lax.broadcasted_iota(jnp.int32, (rows, columns), 1)
    return jnp.where(at == to, 1.0, 0.0).astype(BF16)


def kernel(
    sizes,
    lat_hbm, og_hbm, wq_hbm, wk_hbm, wv_hbm, wo_hbm, gain_hbm,
    out_ref,
    lat_ref, og_ref, wq_ref, wk_ref, wv_ref, wo_ref, gain_ref,
    xt_all, og_all, wkv_all, wqo_all, kv_all, qd_all, st_all,
    xt_own, og_own, gain_own,
    s_ref, dp_ref, kt_ref, ds_ref, s2_ref, dp2_ref, p2_ref, ds2_ref,
    rs_leaf_tx, rs_hub_tx, rs_leaf, rs_hub,
    pw_tx, pw0, pw1, pw2,
    in_sem,
    z_send, z_recv,
    w_send, w_recv, wsib_recv,
    a_send, a_recv, asib_recv,
    st_send, st_recv,
    rs_send, rs_recv,
    p_send, p_recv,
):
    depths, los, ys, zs = sizes
    xs = depths * los
    chips = los * ys
    planes = xs * ys
    rows = chips * 2
    seq = rows * TOK
    quarter = zs // 4

    d = lax.axis_index("depth")
    r = lax.axis_index("row")
    c = lax.axis_index("col")
    core = lax.rem(r, 2)
    other = 1 - core
    chip = r // 2
    lo = chip // ys
    y = lax.rem(chip, ys)
    x = d * los + lo
    here = x * ys + y

    sibling = (d, chip * 2 + other, c)

    def z_at(by):
        return lax.rem(c + by % zs, zs)

    def z_device(by):
        return (d, r, z_at(by))

    def plane_device(at):
        to_x, to_y = at // ys, lax.rem(at, ys)
        return (to_x // los, (lax.rem(to_x, los) * ys + to_y) * 2 + core, c)

    def remote(src, dst, send, recv, device):
        return pltpu.make_async_remote_copy(
            src_ref=src, dst_ref=dst, send_sem=send, recv_sem=recv, device_id=device, device_id_type=MESH
        )

    inputs = (lat_hbm, og_hbm, gain_hbm, wk_hbm, wv_hbm, wq_hbm, wo_hbm)
    staged = (lat_ref, og_ref, gain_ref, wk_ref, wv_ref, wq_ref, wo_ref)
    fetches = [pltpu.make_async_copy(a, b, in_sem.at[i]) for i, (a, b) in enumerate(zip(inputs, staged))]
    for fetch in fetches:
        fetch.start()

    barrier = pltpu.get_barrier_semaphore()

    def greet(device):
        pl.semaphore_signal(barrier, inc=1, device_id=device, device_id_type=MESH)

    for by in sorted({by % zs for by in (1, -1, 2, -2)}):
        greet(z_device(by))
    greet(sibling)

    @pl.loop(1, planes)
    def _(i):
        greet(plane_device(lax.rem(here + i, planes)))

    for fetch in fetches:
        fetch.wait()

    row_at = lax.broadcasted_iota(jnp.int32, (PAD, TOK), 0)
    nothing = jnp.zeros((PAD - FEAT, WIDE), BF16)

    def padded(ref):
        return jnp.concatenate([ref[...], nothing], axis=0)

    og_all[c] = padded(og_ref)
    xt = padded(lat_ref).astype(F32)
    gain_wide = dot_nt(eye(PAD, FEAT) * gain_ref[...].reshape(1, FEAT), jnp.ones((TOK, FEAT), BF16))
    squares = jnp.sum(xt * xt, axis=0, keepdims=True)
    square_hi = squares.astype(BF16).astype(F32)
    rest = squares - square_hi
    square_mid = rest.astype(BF16).astype(F32)
    square_lo = rest - square_mid
    sent = xt * gain_wide
    sent = jnp.where(row_at == FEAT, square_hi, sent)
    sent = jnp.where(row_at == FEAT + 1, square_mid, sent)
    sent = jnp.where(row_at == FEAT + 2, square_lo, sent)
    xt_all[c] = sent.astype(BF16)
    xt_own[...] = xt
    og_own[...] = padded(og_ref).astype(F32)
    gain_own[...] = gain_wide
    wkv_all[lo, y, core] = jnp.concatenate([padded(wk_ref), padded(wv_ref)], axis=1)
    wqo_all[lo, y, core] = jnp.concatenate([padded(wq_ref), padded(wo_ref)], axis=1)

    pl.semaphore_wait(barrier, len({by % zs for by in (1, -1, 2, -2)}) + planes)

    streams = (xt_all, og_all)

    def tree(stream, side, leaf, k):
        sign = -1 if side else 1
        slot = streams[stream].at[z_at(-2 * k * sign)]
        to = z_device(sign if leaf else 2 * sign)
        return remote(slot, slot, z_send.at[stream], z_recv.at[stream, side, leaf, k], to)

    def tree_came(stream, side, leaf, k):
        sign = -1 if side else 1
        slot = streams[stream].at[z_at(-(2 * k + (1 if leaf else 2)) * sign)]
        remote(slot, slot, z_send.at[stream], z_recv.at[stream, side, leaf, k], sibling).wait_recv()

    def tree_round(stream, k):
        if k:
            tree_came(stream, 0, 0, k - 1)
        tree(stream, 0, 0, k).start()
        if k:
            tree(stream, 0, 1, k).start()
            tree_came(stream, 1, 0, k - 1)
        if k < quarter - 1:
            tree(stream, 1, 0, k).start()
        if not k:
            tree(stream, 0, 1, k).start()
        tree(stream, 1, 1, k).start()

    def tree_end(stream):
        tree_came(stream, 0, 0, quarter - 1)
        for k in range(quarter):
            tree_came(stream, 0, 1, k)
            tree_came(stream, 1, 1, k)

    def column_device(up):
        return (d, (lo * ys + lax.rem(y + up % ys, ys)) * 2 + core, c)

    def x_device(by):
        return plane_device(lax.rem(x + by % xs, xs) * ys + y)

    def y_at(up):
        return lax.rem(y + up % ys, ys)

    weights = (wkv_all, wqo_all)

    def weight_y(array, up, start, size, to):
        slot = weights[array].at[lo, y_at(up), core, pl.ds(start, size)]
        return remote(slot, slot, w_send.at[array, 0], w_recv.at[array, y_at(up)], column_device(to))

    def weight_y_came(array, up):
        weight_y(array, up, 0, PAD, 0).wait_recv()

    def weight_x(array, side):
        slot = weights[array].at[lo, :, core, pl.ds(side * HALF, HALF)]
        return remote(slot, slot, w_send.at[array, 1], w_recv.at[array, ys], x_device(-1 if side else 1))

    def weight_x_one(array, up):
        for side in range(2):
            slot = weights[array].at[lo, y_at(up), core, pl.ds(side * HALF, HALF)]
            to = x_device(-1 if side else 1)
            remote(slot, slot, w_send.at[array, 1], w_recv.at[array, ys], to).start()

    def weight_sibling(array, of_lo):
        slot = weights[array].at[of_lo, :, core]
        return remote(slot, slot, w_send.at[array, 2], wsib_recv.at[array], sibling)

    def weight_first(array):
        if ys == 4:
            weight_y(array, 0, 0, PAD, 1).start()
            weight_y(array, 0, 0, PAD, -1).start()
        elif ys == 2:
            weight_y(array, 0, 0, PAD, 1).start()

    def weight_near(array):
        if ys == 4:
            weight_y_came(array, -1)
            weight_y(array, -1, 0, HALF, 1).start()
            weight_y_came(array, 1)
            weight_y(array, 1, HALF, HALF, -1).start()
            if array == 0:
                weight_x_one(array, -1)
                weight_x_one(array, 1)
        elif ys == 2:
            weight_y_came(array, 1)
            if array == 0:
                weight_x_one(array, 1)

    def weight_column(array):
        if ys == 4:
            weight_y_came(array, 2)
            if array == 0:
                weight_x_one(array, 2)
        if array == 1:
            weight_x(array, 0).start()
            weight_x(array, 1).start()
        weight_sibling(array, lo).start()

    def weight_crossed(array):
        slot = weights[array].at[1 - lo, :, core]
        remote(slot, slot, w_send.at[array, 2], w_recv.at[array, ys], sibling).wait_recv()
        weight_sibling(array, 1 - lo).start()

    def weight_all(array):
        slot = weights[array].at[:, :, other]
        remote(slot, slot, w_send.at[array, 2], wsib_recv.at[array], sibling).wait_recv()

    def sent(ref, sem):
        remote(ref, ref, sem, p_recv.at[0], sibling).wait_send()

    tree_round(0, 0)
    weight_first(0)
    weight_x_one(0, 0)
    weight_first(1)
    for k in range(1, quarter):
        tree_round(0, k)
        if k == 1:
            weight_near(0)
        if k == 2:
            weight_column(0)
            weight_near(1)
    if quarter < 2:
        weight_near(0)
    tree_round(1, 0)
    if quarter < 3:
        weight_column(0)
        weight_near(1)
    weight_column(1)
    weight_crossed(0)
    tree_end(0)
    weight_all(0)
    if quarter > 1:
        tree_round(1, 1)

    tails = jnp.zeros((16, TOK), F32)
    for j in range(zs):
        tails = tails + xt_all[j, PAD - 16 : PAD, :].astype(F32)
    square_sum = jnp.sum(tails[8:16], axis=0, keepdims=True)
    scale_row = lax.rsqrt(square_sum * (1.0 / (zs * FEAT)) + epsilon)
    scale_wide = jnp.transpose(jnp.broadcast_to(scale_row, (TOK, TOK)))
    scale_two = jnp.concatenate([scale_wide, scale_wide], axis=1)
    pair = min(ys, 2)

    def project(source, weight, lanes):
        total = None
        for of_lo in range(los):
            for of_y in range(0, ys, pair):
                first = (of_lo * ys + of_y) * 2
                a = source[first : first + 2 * pair].reshape(2 * pair * PAD, TOK)
                b = weight[of_lo, of_y : of_y + pair, :, :, lanes]
                term = dot_tn(a, b.reshape(2 * pair * PAD, b.shape[-1]))
                total = term if total is None else total + term
        return total

    gathered = (kv_all, qd_all)
    half = TOK // 2

    def column(across):
        return 1 - lo if across else lo

    def slot_x(array):
        slot = gathered[array].at[lo, y, core]
        to = (d, ((1 - lo) * ys + y) * 2 + core, c)
        return remote(slot, slot, a_send.at[array, 1], a_recv.at[array, lo, y], to)

    def slot_y(array, across, up, start, size, to):
        slot = gathered[array].at[column(across), y_at(up), core, pl.ds(start, size)]
        recv = a_recv.at[array, column(across), y_at(up)]
        return remote(slot, slot, a_send.at[array, 0], recv, column_device(to))

    def slot_came(array, across, up):
        slot_y(array, across, up, 0, TOK, 0).wait_recv()

    def slot_out(array, across):
        if across:
            slot_came(array, 1, 0)
        if ys == 4:
            slot_y(array, across, 0, 0, TOK, 1).start()
            slot_y(array, across, 0, 0, TOK, -1).start()
        elif ys == 2:
            slot_y(array, across, 0, 0, TOK, 1).start()

    def slot_start(array):
        slot_x(array).start()
        slot_out(array, 0)

    def slot_near(array, across):
        if ys == 4:
            slot_came(array, across, -1)
            slot_y(array, across, -1, 0, half, 1).start()
            slot_came(array, across, 1)
            slot_y(array, across, 1, half, half, -1).start()
        elif ys == 2:
            slot_came(array, across, 1)

    def slot_far(array, across):
        if ys == 4:
            slot_came(array, across, 2)
        slot = gathered[array].at[column(across), :, core]
        remote(slot, slot, a_send.at[array, 2], asib_recv.at[array], sibling).start()

    def slot_all(array):
        slot = gathered[array].at[:, :, other]
        remote(slot, slot, a_send.at[array, 2], asib_recv.at[array], sibling).wait_recv()

    kv = (project(xt_all, wkv_all, slice(0, SLOT)) * scale_two).astype(BF16)
    kv_all[lo, y, core] = kv
    slot_start(0)
    weight_crossed(1)
    if quarter > 2:
        tree_round(1, 2)
    weight_all(1)
    queries = (project(xt_all, wqo_all, slice(0, WIDE)) * scale_wide).astype(BF16)
    slot_out(0, 1)
    slot_near(0, 0)
    if quarter > 3:
        tree_round(1, 3)
    slot_near(0, 1)
    slot_far(0, 0)
    tree_end(1)
    out_dir = project(og_all, wqo_all, slice(WIDE, SLOT)).astype(BF16)
    scaled_queries = (queries.astype(F32) * 0.125).astype(BF16)
    qd_all[lo, y, core] = jnp.concatenate([scaled_queries, out_dir], axis=1)
    slot_start(1)
    slot_far(0, 1)
    low = lax.broadcasted_iota(jnp.int32, (TOK, WIDE), 1) < HDIM

    def stacked(a):
        wide = a.astype(F32)
        parts = [jnp.where(low, wide, 0.0), jnp.where(low, 0.0, wide)]
        return jnp.concatenate(parts, axis=0).astype(BF16)

    query_stack = stacked(scaled_queries)
    dir_stack = stacked(out_dir)

    def slots_of(ref, parity, lanes):
        return ref[:, :, parity, :, lanes].reshape(chips * TOK, lanes.stop - lanes.start)

    def scores_of(parity):
        keys = slots_of(kv_all, parity, slice(0, WIDE))
        scores = dot_nt(keys, query_stack)
        s_ref[:, :, parity] = scores.reshape(los, ys, TOK, SLOT)
        prob_grad = dot_nt(slots_of(kv_all, parity, slice(WIDE, SLOT)), dir_stack)
        dp_ref[:, :, parity] = prob_grad.reshape(los, ys, TOK, SLOT)
        kt_ref[parity] = jnp.transpose(keys)
        return jnp.max(scores.reshape(chips * TOK // 8, 8, SLOT), axis=0)

    most = scores_of(core)
    slot_out(1, 1)
    slot_near(1, 0)
    slot_all(0)
    most = jnp.max(jnp.maximum(most, scores_of(other)), axis=0, keepdims=True)
    slot_near(1, 1)
    slot_far(1, 0)

    def tile_at(i):
        return i // (2 * ys), lax.rem(i // 2, ys), lax.rem(i, 2)

    def folded(a):
        return jnp.sum(a.reshape(TOK // 8, 8, SLOT), axis=0)

    def expo_body(i, sums):
        at = tile_at(i)
        expo = jnp.exp(s_ref[at] - most)
        s_ref[at] = expo
        return sums[0] + folded(expo), sums[1] + folded(expo * dp_ref[at])

    zero = jnp.zeros((8, SLOT), F32)
    totals, delta = lax.fori_loop(0, rows, expo_body, (zero, zero), unroll=2)
    totals = jnp.sum(totals, axis=0, keepdims=True)
    inverse = 1.0 / totals
    delta = jnp.sum(delta, axis=0, keepdims=True) * inverse
    slot_far(1, 1)

    def stat_copy(i):
        to = lax.rem(r + i, rows)
        return remote(st_all.at[r], st_all.at[r], st_send, st_recv, (d, to, c))

    def small_came(ref, count, sem):
        some = ref.at[pl.ds(0, count)]
        remote(some, some, p_send.at[0], sem, sibling).wait_recv()

    st_all[r] = jnp.concatenate([most + jnp.log(totals), delta, jnp.zeros((6, SLOT), F32)], axis=0)

    @pl.loop(1, rows)
    def _(i):
        stat_copy(i).start()

    def score_grad_body(i, nothing):
        at = tile_at(i)
        ds_ref[at] = (s_ref[at] * (dp_ref[at] - delta)).astype(BF16)
        return nothing

    lax.fori_loop(0, rows, score_grad_body, 0, unroll=2)
    query_grad = jnp.zeros((WIDE, SLOT), F32)
    for parity in range(2):
        query_grad = query_grad + dot_nn(kt_ref[parity], slots_of(ds_ref, parity, slice(0, SLOT)))
    query_grad = query_grad * (inverse * 0.125)
    query_grad = jnp.concatenate([query_grad[0:HDIM, 0:TOK], query_grad[HDIM:WIDE, TOK:SLOT]], axis=0)
    query_grad = query_grad.astype(BF16)

    key_stack = stacked(kv[:, 0:WIDE])
    value_stack = stacked(kv[:, WIDE:SLOT])
    wide = pair * TOK
    blocks = [(of_lo, of_y) for of_lo in range(los) for of_y in range(0, ys, pair)]
    parities = (core, other)

    def own_scores(side):
        for n, (of_lo, of_y) in enumerate(blocks):
            block = qd_all[of_lo, of_y : of_y + pair, parities[side]].reshape(wide, SLOT)
            s2_ref[side * len(blocks) + n] = dot_nt(key_stack, block[:, 0:WIDE])
            dp2_ref[side * len(blocks) + n] = dot_nt(value_stack, block[:, WIDE:SLOT])

    own_scores(0)
    slot_all(1)
    own_scores(1)
    small_came(st_all, rows - 1, st_recv)

    for side in range(2):
        for n, (of_lo, of_y) in enumerate(blocks):
            stats = [st_all[(of_lo * ys + of_y + i) * 2 + parities[side]] for i in range(pair)]
            at = side * len(blocks) + n
            lanes = slice(at * wide, (at + 1) * wide)
            for head in range(2):
                part = slice(head * TOK, (head + 1) * TOK)
                total = jnp.concatenate([stat[0:1, part] for stat in stats], axis=1)
                shift = jnp.concatenate([stat[1:2, part] for stat in stats], axis=1)
                probs = jnp.exp(s2_ref[at, part] - total)
                p2_ref[part, lanes] = probs.astype(BF16)
                ds2_ref[part, lanes] = (probs * (dp2_ref[at, part] - shift)).astype(BF16)

    key_grad = jnp.zeros((SLOT, WIDE), F32)
    value_grad = jnp.zeros((SLOT, WIDE), F32)
    for side in range(2):
        lanes = slice(side * chips * TOK, (side + 1) * chips * TOK)
        key_grad = key_grad + dot_nn(ds2_ref[:, lanes], slots_of(qd_all, parities[side], slice(0, WIDE)))
        value_grad = value_grad + dot_nn(p2_ref[:, lanes], slots_of(qd_all, parities[side], slice(WIDE, SLOT)))
    key_grad = jnp.where(low, key_grad[0:TOK], key_grad[TOK:SLOT])
    value_grad = jnp.where(low, value_grad[0:TOK], value_grad[TOK:SLOT])
    kv_grad = jnp.concatenate([key_grad, value_grad], axis=1)
    turned = jnp.concatenate([jnp.transpose(key_grad), jnp.transpose(value_grad)], axis=0).astype(BF16)
    kv_grad = kv_grad.astype(BF16)
    grads_turned = jnp.concatenate([turned, query_grad], axis=0)

    queries_turned = dot_nt(eye(WIDE, WIDE), queries)
    inner = jnp.sum(query_grad.astype(F32) * queries_turned, axis=0, keepdims=True)
    kv_inner = kv_grad.astype(F32) * kv.astype(F32)
    kv_hi = kv_inner.astype(BF16)
    kv_lo = (kv_inner - kv_hi.astype(F32)).astype(BF16)
    ones = jnp.ones((8, SLOT), BF16)
    kv_inner = dot_nt(ones, kv_hi) + dot_nt(ones, kv_lo)
    inner = inner + kv_inner[0:1]

    def partials(places):
        slots = []
        for by in places:
            j = z_at(by)
            at = (j // (2 * ys), lax.rem(j // 2, ys), lax.rem(j, 2))
            slots.append(jnp.concatenate([wkv_all[at], wqo_all[at + (slice(None), slice(0, WIDE))]], axis=1))
        value = dot_nn(jnp.concatenate(slots, axis=0), grads_turned)
        parts = [value[i * PAD : (i + 1) * PAD] for i in range(len(places))]
        return [jnp.where(row_at == FEAT, inner, part) for part in parts]

    some = pl.ds(0, zs - 1)
    for i in range(2):
        sent(streams[i].at[some], z_send.at[i])
        for group, sems, x_slots in ((weights[i], w_send, slice(0, ys)), (gathered[i], a_send, slice(0, 1))):
            if ys > 1:
                columns = slice(0, 1) if group is weights[i] else slice(0, 2)
                sent(group.at[columns, pl.ds(0, ys - 1), 0], sems.at[i, 0])
            sent(group.at[0, x_slots, 0], sems.at[i, 1])
            sent(group.at[:, :, 0], sems.at[i, 2])

    sent(st_all.at[pl.ds(0, rows - 1)], st_send)

    far = 2 * quarter

    def rs_leaf_copy(side, m):
        to = z_device(-1 if side else 1)
        return remote(rs_leaf_tx.at[side, m], rs_leaf.at[side, m], rs_send.at[side], rs_recv.at[side, 1, m], to)

    def rs_hub_copy(side, k):
        to = z_device(-2 if side else 2)
        return remote(rs_hub_tx.at[side, k], rs_hub.at[side, k], rs_send.at[side], rs_recv.at[side, 0, k], to)

    def leaf(side, m, part):
        rs_leaf_tx[side, m] = part.astype(BF16)
        rs_leaf_copy(side, m).start()

    hub_part, right_part, left_part = partials([far, far - 1, 1 - far])
    rs_hub_tx[0, 0] = hub_part.astype(BF16)
    rs_hub_copy(0, 0).start()
    leaf(0, 0, right_part)
    leaf(1, 0, left_part)
    for k in range(1, quarter):
        by = far - 2 * k
        to_right, to_left, right_part, left_part = partials([by, -by, by - 1, 1 - by])
        rs_hub_copy(0, k - 1).wait_recv()
        rs_leaf_copy(0, k - 1).wait_recv()
        total = to_right + rs_hub[0, k - 1].astype(F32) + rs_leaf[0, k - 1].astype(F32)
        rs_hub_tx[0, k] = total.astype(BF16)
        rs_hub_copy(0, k).start()
        rs_leaf_copy(1, k - 1).wait_recv()
        total = to_left + rs_leaf[1, k - 1].astype(F32)
        if k > 1:
            rs_hub_copy(1, k - 2).wait_recv()
            total = total + rs_hub[1, k - 2].astype(F32)
        rs_hub_tx[1, k - 1] = total.astype(BF16)
        rs_hub_copy(1, k - 1).start()
        leaf(0, k, right_part)
        leaf(1, k, left_part)

    own = partials([0])[0]
    for side in range(2):
        last = quarter - 1 - side
        rs_leaf_copy(side, quarter - 1).wait_recv()
        own = own + rs_leaf[side, quarter - 1].astype(F32)
        if last >= 0:
            rs_hub_copy(side, last).wait_recv()
            own = own + rs_hub[side, last].astype(F32)

    inner = own[FEAT : FEAT + 1] * (1.0 / (zs * FEAT))
    scaled = own * gain_own[...]
    normalized = xt_own[...] * scale_row
    raw = og_own[...] + scale_row * (scaled - normalized * inner)
    power = jnp.sum((raw * raw).reshape(PAD // 8, 8, TOK), axis=0)

    def power_sibling():
        return remote(pw_tx.at[0], pw0, p_send.at[0], p_recv.at[0], sibling)

    def power_plane(i):
        to = plane_device(lax.rem(here + i, planes))
        return remote(pw_tx.at[1], pw1.at[here], p_send.at[1], p_recv.at[1], to)

    def power_col(i):
        return remote(pw_tx.at[2], pw2.at[c], p_send.at[2], p_recv.at[2], (d, r, lax.rem(c + i, zs)))

    pw_tx[0] = power
    power_sibling().start()
    power_sibling().wait_recv()
    power = power + pw0[...]
    pw_tx[1] = power
    pw1[here] = power

    @pl.loop(1, planes)
    def _(i):
        power_plane(i).start()

    small_came(pw1, planes - 1, p_recv.at[1])

    sent(xt_all.at[pl.ds(0, far)], rs_send.at[0])
    sent(xt_all.at[pl.ds(0, far - 1)], rs_send.at[1])
    power = jnp.sum(pw1[...], axis=0)
    pw_tx[2] = power
    pw2[c] = power

    @pl.loop(1, zs)
    def _(i):
        power_col(i).start()

    small_came(pw2, zs - 1, p_recv.at[2])

    power_sibling().wait_send()
    sent(pw1.at[pl.ds(0, planes - 1)], p_send.at[1])
    sent(pw2.at[pl.ds(0, zs - 1)], p_send.at[2])
    power = jnp.sum(jnp.sum(pw2[...], axis=0), axis=0, keepdims=True)
    power = jnp.sum(power, axis=1, keepdims=True)
    cells = depths * seq * zs * FEAT
    final = raw * lax.rsqrt(power * (1.0 / cells) + epsilon)
    out_ref[...] = final[0:FEAT].astype(BF16)


def sizes_of(mesh):
    depths, rows, zs = mesh.shape["depth"], mesh.shape["row"], mesh.shape["col"]
    los = 2
    return depths, los, rows // (2 * los), zs


def solution(mesh):
    depths, los, ys, zs = sizes_of(mesh)
    chips, planes = los * ys, depths * los * ys
    rows = chips * 2
    quarter = zs // 4
    dma = pltpu.SemaphoreType.DMA
    scratch = [
        *([pltpu.VMEM((FEAT, TOK), BF16)] * 6),
        pltpu.VMEM((FEAT,), BF16),
        pltpu.VMEM((zs, PAD, TOK), BF16),
        pltpu.VMEM((zs, PAD, TOK), BF16),
        pltpu.VMEM((los, ys, 2, PAD, SLOT), BF16),
        pltpu.VMEM((los, ys, 2, PAD, SLOT), BF16),
        pltpu.VMEM((los, ys, 2, TOK, SLOT), BF16),
        pltpu.VMEM((los, ys, 2, TOK, SLOT), BF16),
        pltpu.VMEM((rows, 8, SLOT), F32),
        pltpu.VMEM((PAD, TOK), F32),
        pltpu.VMEM((PAD, TOK), F32),
        pltpu.VMEM((PAD, TOK), F32),
        pltpu.VMEM((los, ys, 2, TOK, SLOT), F32),
        pltpu.VMEM((los, ys, 2, TOK, SLOT), F32),
        pltpu.VMEM((2, WIDE, chips * TOK), BF16),
        pltpu.VMEM((los, ys, 2, TOK, SLOT), BF16),
        pltpu.VMEM((rows // min(ys, 2), SLOT, min(ys, 2) * TOK), F32),
        pltpu.VMEM((rows // min(ys, 2), SLOT, min(ys, 2) * TOK), F32),
        pltpu.VMEM((SLOT, rows * TOK), BF16),
        pltpu.VMEM((SLOT, rows * TOK), BF16),
        *([pltpu.VMEM((2, quarter, PAD, TOK), BF16)] * 4),
        pltpu.VMEM((3, 8, TOK), F32),
        pltpu.VMEM((8, TOK), F32),
        pltpu.VMEM((planes, 8, TOK), F32),
        pltpu.VMEM((zs, 8, TOK), F32),
        dma((7,)),
        dma((2,)), dma((2, 2, 2, quarter)),
        dma((2, 3)), dma((2, ys + 1)), dma((2,)),
        dma((2, 3)), dma((2, los, ys)), dma((2,)),
        dma, dma,
        dma((2,)), dma((2, 2, quarter)),
        dma((3,)), dma((3,)),
    ]

    def shards(latents, out_grad, w_query, w_key, w_value, w_out, gain):
        return pl.pallas_call(
            functools.partial(kernel, (depths, los, ys, zs)),
            out_shape=jax.ShapeDtypeStruct((FEAT, TOK), BF16),
            in_specs=[pl.BlockSpec(memory_space=pl.ANY)] * 7,
            out_specs=pl.BlockSpec(memory_space=pltpu.VMEM),
            scratch_shapes=scratch,
            compiler_params=pltpu.CompilerParams(
                collective_id=0, has_side_effects=True, vmem_limit_bytes=56 * 1024 * 1024
            ),
        )(latents.T, out_grad.T, w_query, w_key, w_value, w_out, gain).T

    return jax.shard_map(
        shards,
        mesh=mesh,
        in_specs=(
            P(("depth", "row"), "col"),
            P(("depth", "row"), "col"),
            P("row", "col"),
            P("row", "col"),
            P("row", "col"),
            P("row", "col"),
            P("col"),
        ),
        out_specs=P(("depth", "row"), "col"),
        check_vma=False,
    )
```

time: 578 us -> 98 us (0.17)
  blocking collectives: 346 us -> 0 us
  waiting for transfers between devices: 190 us -> 0 us
  Pallas kernels: 0 us -> 96.3 us
  between operations: 14 us -> 0.01 us
  matrix products: 13.5 us -> 0 us
  other arithmetic: 7.68 us -> 0 us
    unnamed x6 -> x0, waiting for transfers between devices: 190 us -> none
    all_gather x8 -> x0, blocking collectives: 175 us -> none  [the longest x1 36.3 us: shards(): lax.all_gather(w_query, 'row', axis=0, tiled=True)]
    psum x3 -> x0, blocking collectives: 171 us -> none  [the longest x1 119 us: shards(): grad_power = lax.psum(jnp.sum(raw * raw), ('depth', 'row', 'col'))]
    pallas_call x0 -> x1, Pallas kernels: none -> 96.3 us  [shards(): pl.pallas_call(functools.partial(kernel, (depths, los, ys, zs)), out_shap...]
    dot_general x19 -> x0, matrix products: 13.5 us -> none  [the longest x1 1.9 us: shards(): jnp.einsum('ti,di->td', value_grad, pieces[2], preferred_element_type=jnp...]
  transfers between devices with their start and end apart: 3 -> 0, of which waited for: 3 -> 0; matrix products, arithmetic and copies ran while one was open for 1% -> 0% of each run, Pallas kernels for 0% -> 0%
where the time goes in v2:
time: 98 us; the launch traced here: 97.7 us
  Pallas kernels  96.3 us (98%)
  local copies, waits for them, and re-layouts  1.39 us (1%)
    pallas_call x1, Pallas kernels, shards(): pl.pallas_call(functools.partial(kernel, (depths, los, ys, zs)), out_shap...  96.3 us

profile of v2, /device:TPU:1, one launch (start us, length us, event | category | flops | bytes accessed | tf_op | source)
XLA Modules:
  0.0 97.7 jit_solution(1234977508214137538)
XLA Ops:
  0.0 96.3 %shard_map.73 = bf16[152,128]{1,0:T(8,128)(2,1)} custom-call(bf16[152,128]{1,0:T(8,128)(2,1)} %bitcast.4, bf16[152,128]{1,0:T(8,128)(2,1)} %bitcast.5, bf16[152,128]{1,0:T(8,128)(2,1)} %wq_hbm.1, bf16[152,128]{1,0:T(8,128)(2,1)} %wk_hbm.1, bf16[152,128]{1,0:T(8,128)(2,1)} %wv_hbm.1, bf16[152,128]{1,0:T(8,128)(2,1)} %wo_hbm.1, bf16[152]{0:T(256)(128)(2,1)} %gain_hbm.1), custom_call_target="tpu_custom_call" | custom-call | tf_op jit(solution)/shard_map/pallas_call | solution.py:661
  96.3 1.4 %copy.9 = bf16[128,152]{0,1:T(8,128)(2,1)} copy(bf16[128,152]{0,1:T(8,128)(2,1)} %bitcast.3) | data formatting | bytes 77824

commit v3 on v2

--- a/solution.py
+++ b/solution.py
@@ -45,7 +45,7 @@
     lat_ref, og_ref, wq_ref, wk_ref, wv_ref, wo_ref, gain_ref,
     xt_all, og_all, wkv_all, wqo_all, kv_all, qd_all, st_all,
     xt_own, og_own, gain_own,
-    s_ref, dp_ref, kt_ref, ds_ref, s2_ref, dp2_ref, p2_ref, ds2_ref,
+    s_ref, dp_ref, kt_ref, ds_ref, s2_ref, dp2_ref,
     rs_leaf_tx, rs_hub_tx, rs_leaf, rs_hub,
     pw_tx, pw0, pw1, pw2,
     in_sem,
@@ -281,16 +281,21 @@
     scale_two = jnp.concatenate([scale_wide, scale_wide], axis=1)
     pair = min(ys, 2)
 
+    pairs = ys // pair
+
+    def pair_at(n):
+        return n // pairs, pl.ds(lax.rem(n, pairs) * pair, pair)
+
     def project(source, weight, lanes):
-        total = None
-        for of_lo in range(los):
-            for of_y in range(0, ys, pair):
-                first = (of_lo * ys + of_y) * 2
-                a = source[first : first + 2 * pair].reshape(2 * pair * PAD, TOK)
-                b = weight[of_lo, of_y : of_y + pair, :, :, lanes]
-                term = dot_tn(a, b.reshape(2 * pair * PAD, b.shape[-1]))
-                total = term if total is None else total + term
-        return total
+        width = lanes.stop - lanes.start
+
+        def body(n, total):
+            of_lo, of_ys = pair_at(n)
+            a = source[pl.ds(n * 2 * pair, 2 * pair)].reshape(2 * pair * PAD, TOK)
+            b = weight[of_lo, of_ys, :, :, lanes].reshape(2 * pair * PAD, width)
+            return total + dot_tn(a, b)
+
+        return lax.fori_loop(0, los * pairs, body, jnp.zeros((TOK, width), F32))
 
     gathered = (kv_all, qd_all)
     half = TOK // 2
@@ -442,39 +447,45 @@
     key_stack = stacked(kv[:, 0:WIDE])
     value_stack = stacked(kv[:, WIDE:SLOT])
     wide = pair * TOK
-    blocks = [(of_lo, of_y) for of_lo in range(los) for of_y in range(0, ys, pair)]
+    blocks = los * pairs
     parities = (core, other)
 
+    def block_of(n, parity):
+        of_lo, of_ys = pair_at(n)
+        return qd_all[of_lo, of_ys, parity].reshape(wide, SLOT)
+
     def own_scores(side):
-        for n, (of_lo, of_y) in enumerate(blocks):
-            block = qd_all[of_lo, of_y : of_y + pair, parities[side]].reshape(wide, SLOT)
-            s2_ref[side * len(blocks) + n] = dot_nt(key_stack, block[:, 0:WIDE])
-            dp2_ref[side * len(blocks) + n] = dot_nt(value_stack, block[:, WIDE:SLOT])
+        @pl.loop(0, blocks)
+        def _(n):
+            block = block_of(n, parities[side])
+            s2_ref[side * blocks + n] = dot_nt(key_stack, block[:, 0:WIDE])
+            dp2_ref[side * blocks + n] = dot_nt(value_stack, block[:, WIDE:SLOT])
 
     own_scores(0)
     slot_all(1)
     own_scores(1)
     small_came(st_all, rows - 1, st_recv)
 
-    for side in range(2):
-        for n, (of_lo, of_y) in enumerate(blocks):
-            stats = [st_all[(of_lo * ys + of_y + i) * 2 + parities[side]] for i in range(pair)]
-            at = side * len(blocks) + n
-            lanes = slice(at * wide, (at + 1) * wide)
-            for head in range(2):
-                part = slice(head * TOK, (head + 1) * TOK)
-                total = jnp.concatenate([stat[0:1, part] for stat in stats], axis=1)
-                shift = jnp.concatenate([stat[1:2, part] for stat in stats], axis=1)
-                probs = jnp.exp(s2_ref[at, part] - total)
-                p2_ref[part, lanes] = probs.astype(BF16)
-                ds2_ref[part, lanes] = (probs * (dp2_ref[at, part] - shift)).astype(BF16)
-
-    key_grad = jnp.zeros((SLOT, WIDE), F32)
-    value_grad = jnp.zeros((SLOT, WIDE), F32)
-    for side in range(2):
-        lanes = slice(side * chips * TOK, (side + 1) * chips * TOK)
-        key_grad = key_grad + dot_nn(ds2_ref[:, lanes], slots_of(qd_all, parities[side], slice(0, WIDE)))
-        value_grad = value_grad + dot_nn(p2_ref[:, lanes], slots_of(qd_all, parities[side], slice(WIDE, SLOT)))
+    def key_body(at, grads):
+        parity = jnp.where(at < blocks, core, other)
+        n = lax.rem(at, blocks)
+        first = (n // pairs) * ys + lax.rem(n, pairs) * pair
+        stats = [st_all[(first + i) * 2 + parity] for i in range(pair)]
+        probs, score_grad = [], []
+        for head in range(2):
+            part = slice(head * TOK, (head + 1) * TOK)
+            total = jnp.concatenate([stat[0:1, part] for stat in stats], axis=1)
+            shift = jnp.concatenate([stat[1:2, part] for stat in stats], axis=1)
+            prob = jnp.exp(s2_ref[at, part] - total)
+            probs.append(prob.astype(BF16))
+            score_grad.append((prob * (dp2_ref[at, part] - shift)).astype(BF16))
+        block = block_of(n, parity)
+        key_grad = grads[0] + dot_nn(jnp.concatenate(score_grad, axis=0), block[:, 0:WIDE])
+        value_grad = grads[1] + dot_nn(jnp.concatenate(probs, axis=0), block[:, WIDE:SLOT])
+        return key_grad, value_grad
+
+    zero = jnp.zeros((SLOT, WIDE), F32)
+    key_grad, value_grad = lax.fori_loop(0, 2 * blocks, key_body, (zero, zero))
     key_grad = jnp.where(low, key_grad[0:TOK], key_grad[TOK:SLOT])
     value_grad = jnp.where(low, value_grad[0:TOK], value_grad[TOK:SLOT])
     kv_grad = jnp.concatenate([key_grad, value_grad], axis=1)
@@ -494,7 +505,7 @@
     def partials(places):
         slots = []
         for by in places:
-            j = z_at(by)
+            j = lax.rem(c + by + zs, zs)
             at = (j // (2 * ys), lax.rem(j // 2, ys), lax.rem(j, 2))
             slots.append(jnp.concatenate([wkv_all[at], wqo_all[at + (slice(None), slice(0, WIDE))]], axis=1))
         value = dot_nn(jnp.concatenate(slots, axis=0), grads_turned)
@@ -517,47 +528,55 @@
 
     def rs_leaf_copy(side, m):
         to = z_device(-1 if side else 1)
-        return remote(rs_leaf_tx.at[side, m], rs_leaf.at[side, m], rs_send.at[side], rs_recv.at[side, 1, m], to)
+        return remote(rs_leaf_tx.at[side, m], rs_leaf.at[side, m + 1], rs_send.at[side], rs_recv.at[side, 1, m], to)
 
     def rs_hub_copy(side, k):
         to = z_device(-2 if side else 2)
-        return remote(rs_hub_tx.at[side, k], rs_hub.at[side, k], rs_send.at[side], rs_recv.at[side, 0, k], to)
-
-    def leaf(side, m, part):
-        rs_leaf_tx[side, m] = part.astype(BF16)
-        rs_leaf_copy(side, m).start()
-
-    hub_part, right_part, left_part = partials([far, far - 1, 1 - far])
-    rs_hub_tx[0, 0] = hub_part.astype(BF16)
-    rs_hub_copy(0, 0).start()
-    leaf(0, 0, right_part)
-    leaf(1, 0, left_part)
-    for k in range(1, quarter):
+        return remote(rs_hub_tx.at[side, k], rs_hub.at[side, k + 1], rs_send.at[side], rs_recv.at[side, 0, k], to)
+
+    for side in range(2):
+        rs_hub[side, 0] = jnp.zeros((PAD, TOK), BF16)
+        rs_leaf[side, 0] = jnp.zeros((PAD, TOK), BF16)
+
+    @pl.loop(0, quarter)
+    def _(k):
         by = far - 2 * k
         to_right, to_left, right_part, left_part = partials([by, -by, by - 1, 1 - by])
-        rs_hub_copy(0, k - 1).wait_recv()
-        rs_leaf_copy(0, k - 1).wait_recv()
-        total = to_right + rs_hub[0, k - 1].astype(F32) + rs_leaf[0, k - 1].astype(F32)
+
+        @pl.when(k > 0)
+        def _():
+            rs_hub_copy(0, k - 1).wait_recv()
+            rs_leaf_copy(0, k - 1).wait_recv()
+
+        total = to_right + rs_hub[0, k].astype(F32) + rs_leaf[0, k].astype(F32)
         rs_hub_tx[0, k] = total.astype(BF16)
         rs_hub_copy(0, k).start()
-        rs_leaf_copy(1, k - 1).wait_recv()
-        total = to_left + rs_leaf[1, k - 1].astype(F32)
-        if k > 1:
-            rs_hub_copy(1, k - 2).wait_recv()
-            total = total + rs_hub[1, k - 2].astype(F32)
-        rs_hub_tx[1, k - 1] = total.astype(BF16)
-        rs_hub_copy(1, k - 1).start()
-        leaf(0, k, right_part)
-        leaf(1, k, left_part)
+        rs_leaf_tx[0, k] = right_part.astype(BF16)
+        rs_leaf_tx[1, k] = left_part.astype(BF16)
+
+        @pl.when(k > 0)
+        def _():
+            rs_leaf_copy(1, k - 1).wait_recv()
+
+            @pl.when(k > 1)
+            def _():
+                rs_hub_copy(1, k - 2).wait_recv()
+
+            total = to_left + rs_leaf[1, k].astype(F32) + rs_hub[1, k - 1].astype(F32)
+            rs_hub_tx[1, k - 1] = total.astype(BF16)
+            rs_hub_copy(1, k - 1).start()
+
+        rs_leaf_copy(0, k).start()
+        rs_leaf_copy(1, k).start()
 
     own = partials([0])[0]
     for side in range(2):
         last = quarter - 1 - side
         rs_leaf_copy(side, quarter - 1).wait_recv()
-        own = own + rs_leaf[side, quarter - 1].astype(F32)
+        own = own + rs_leaf[side, quarter].astype(F32)
         if last >= 0:
             rs_hub_copy(side, last).wait_recv()
-            own = own + rs_hub[side, last].astype(F32)
+            own = own + rs_hub[side, last + 1].astype(F32)
 
     inner = own[FEAT : FEAT + 1] * (1.0 / (zs * FEAT))
     scaled = own * gain_own[...]
@@ -641,9 +660,8 @@
         pltpu.VMEM((los, ys, 2, TOK, SLOT), BF16),
         pltpu.VMEM((rows // min(ys, 2), SLOT, min(ys, 2) * TOK), F32),
         pltpu.VMEM((rows // min(ys, 2), SLOT, min(ys, 2) * TOK), F32),
-        pltpu.VMEM((SLOT, rows * TOK), BF16),
-        pltpu.VMEM((SLOT, rows * TOK), BF16),
-        *([pltpu.VMEM((2, quarter, PAD, TOK), BF16)] * 4),
+        *([pltpu.VMEM((2, quarter, PAD, TOK), BF16)] * 2),
+        *([pltpu.VMEM((2, quarter + 1, PAD, TOK), BF16)] * 2),
         pltpu.VMEM((3, 8, TOK), F32),
         pltpu.VMEM((8, TOK), F32),
         pltpu.VMEM((planes, 8, TOK), F32),

time: 98 us -> 100 us (1.020)
  Pallas kernels: 96.3 us -> 98.5 us
    pallas_call x1, Pallas kernels: 96.3 us -> 98.5 us  [shards(): pl.pallas_call(functools.partial(kernel, (depths, los, ys, zs)), out_shap...]
where the time goes in v3:
time: 100 us; the launch traced here: 99.9 us
  Pallas kernels  98.5 us (98%)
  local copies, waits for them, and re-layouts  1.39 us (1%)
    pallas_call x1, Pallas kernels, shards(): pl.pallas_call(functools.partial(kernel, (depths, los, ys, zs)), out_shap...  98.5 us

profile of v3, /device:TPU:1, one launch (start us, length us, event | category | flops | bytes accessed | tf_op | source)
XLA Modules:
  0.0 99.9 jit_solution(15947340764755876797)
XLA Ops:
  0.0 98.5 %shard_map.73 = bf16[152,128]{1,0:T(8,128)(2,1)} custom-call(bf16[152,128]{1,0:T(8,128)(2,1)} %bitcast.4, bf16[152,128]{1,0:T(8,128)(2,1)} %bitcast.5, bf16[152,128]{1,0:T(8,128)(2,1)} %wq_hbm.1, bf16[152,128]{1,0:T(8,128)(2,1)} %wk_hbm.1, bf16[152,128]{1,0:T(8,128)(2,1)} %wv_hbm.1, bf16[152,128]{1,0:T(8,128)(2,1)} %wo_hbm.1, bf16[152]{0:T(256)(128)(2,1)} %gain_hbm.1), custom_call_target="tpu_custom_call" | custom-call | tf_op jit(solution)/shard_map/pallas_call | solution.py:679
  98.5 1.4 %copy.9 = bf16[128,152]{0,1:T(8,128)(2,1)} copy(bf16[128,152]{0,1:T(8,128)(2,1)} %bitcast.3) | data formatting | bytes 77824

commit v4 on v2

--- a/solution.py
+++ b/solution.py
@@ -47,7 +47,7 @@
     xt_own, og_own, gain_own,
     s_ref, dp_ref, kt_ref, ds_ref, s2_ref, dp2_ref, p2_ref, ds2_ref,
     rs_leaf_tx, rs_hub_tx, rs_leaf, rs_hub,
-    pw_tx, pw0, pw1, pw2,
+    pw_tx, pw1, pw2,
     in_sem,
     z_send, z_recv,
     w_send, w_recv, wsib_recv,
@@ -111,8 +111,8 @@
     def _(i):
         greet(plane_device(lax.rem(here + i, planes)))
 
-    for fetch in fetches:
-        fetch.wait()
+    fetches[0].wait()
+    fetches[2].wait()
 
     row_at = lax.broadcasted_iota(jnp.int32, (PAD, TOK), 0)
     nothing = jnp.zeros((PAD - FEAT, WIDE), BF16)
@@ -120,7 +120,6 @@
     def padded(ref):
         return jnp.concatenate([ref[...], nothing], axis=0)
 
-    og_all[c] = padded(og_ref)
     xt = padded(lat_ref).astype(F32)
     gain_wide = dot_nt(eye(PAD, FEAT) * gain_ref[...].reshape(1, FEAT), jnp.ones((TOK, FEAT), BF16))
     squares = jnp.sum(xt * xt, axis=0, keepdims=True)
@@ -134,11 +133,7 @@
     sent = jnp.where(row_at == FEAT + 2, square_lo, sent)
     xt_all[c] = sent.astype(BF16)
     xt_own[...] = xt
-    og_own[...] = padded(og_ref).astype(F32)
     gain_own[...] = gain_wide
-    wkv_all[lo, y, core] = jnp.concatenate([padded(wk_ref), padded(wv_ref)], axis=1)
-    wqo_all[lo, y, core] = jnp.concatenate([padded(wq_ref), padded(wo_ref)], axis=1)
-
     pl.semaphore_wait(barrier, len({by % zs for by in (1, -1, 2, -2)}) + planes)
 
     streams = (xt_all, og_all)
@@ -249,25 +244,31 @@
         remote(ref, ref, sem, p_recv.at[0], sibling).wait_send()
 
     tree_round(0, 0)
+    fetches[3].wait()
+    fetches[4].wait()
+    wkv_all[lo, y, core] = jnp.concatenate([padded(wk_ref), padded(wv_ref)], axis=1)
     weight_first(0)
     weight_x_one(0, 0)
-    weight_first(1)
+    for i in (1, 5, 6):
+        fetches[i].wait()
+    wqo_all[lo, y, core] = jnp.concatenate([padded(wq_ref), padded(wo_ref)], axis=1)
+    og_own[...] = padded(og_ref).astype(F32)
+    og_all[c] = padded(og_ref)
     for k in range(1, quarter):
         tree_round(0, k)
         if k == 1:
             weight_near(0)
         if k == 2:
             weight_column(0)
-            weight_near(1)
     if quarter < 2:
         weight_near(0)
-    tree_round(1, 0)
     if quarter < 3:
         weight_column(0)
-        weight_near(1)
-    weight_column(1)
+    weight_first(1)
+    tree_round(1, 0)
     weight_crossed(0)
     tree_end(0)
+    weight_near(1)
     weight_all(0)
     if quarter > 1:
         tree_round(1, 1)
@@ -346,16 +347,17 @@
     kv = (project(xt_all, wkv_all, slice(0, SLOT)) * scale_two).astype(BF16)
     kv_all[lo, y, core] = kv
     slot_start(0)
-    weight_crossed(1)
+    weight_column(1)
     if quarter > 2:
         tree_round(1, 2)
-    weight_all(1)
-    queries = (project(xt_all, wqo_all, slice(0, WIDE)) * scale_wide).astype(BF16)
     slot_out(0, 1)
     slot_near(0, 0)
+    weight_crossed(1)
     if quarter > 3:
         tree_round(1, 3)
     slot_near(0, 1)
+    weight_all(1)
+    queries = (project(xt_all, wqo_all, slice(0, WIDE)) * scale_wide).astype(BF16)
     slot_far(0, 0)
     tree_end(1)
     out_dir = project(og_all, wqo_all, slice(WIDE, SLOT)).astype(BF16)
@@ -418,7 +420,7 @@
 
     def small_came(ref, count, sem):
         some = ref.at[pl.ds(0, count)]
-        remote(some, some, p_send.at[0], sem, sibling).wait_recv()
+        remote(some, some, p_send.at[1], sem, sibling).wait_recv()
 
     st_all[r] = jnp.concatenate([most + jnp.log(totals), delta, jnp.zeros((6, SLOT), F32)], axis=0)
 
@@ -566,27 +568,27 @@
     power = jnp.sum((raw * raw).reshape(PAD // 8, 8, TOK), axis=0)
 
     def power_sibling():
-        return remote(pw_tx.at[0], pw0, p_send.at[0], p_recv.at[0], sibling)
-
-    def power_plane(i):
-        to = plane_device(lax.rem(here + i, planes))
-        return remote(pw_tx.at[1], pw1.at[here], p_send.at[1], p_recv.at[1], to)
+        return remote(pw_tx.at[0], pw1.at[here * 2 + core], p_send.at[0], p_recv.at[0], sibling)
+
+    def power_plane(i, of_core):
+        to = lax.rem(here + i, planes)
+        to_d, to_r, to_c = plane_device(to)
+        to_r = to_r - core + of_core
+        return remote(pw_tx.at[0], pw1.at[here * 2 + core], p_send.at[0], p_recv.at[0], (to_d, to_r, to_c))
 
     def power_col(i):
         return remote(pw_tx.at[2], pw2.at[c], p_send.at[2], p_recv.at[2], (d, r, lax.rem(c + i, zs)))
 
     pw_tx[0] = power
+    pw1[here * 2 + core] = power
     power_sibling().start()
-    power_sibling().wait_recv()
-    power = power + pw0[...]
-    pw_tx[1] = power
-    pw1[here] = power
 
     @pl.loop(1, planes)
     def _(i):
-        power_plane(i).start()
-
-    small_came(pw1, planes - 1, p_recv.at[1])
+        power_plane(i, 0).start()
+        power_plane(i, 1).start()
+
+    small_came(pw1, 2 * planes - 1, p_recv.at[0])
 
     sent(xt_all.at[pl.ds(0, far)], rs_send.at[0])
     sent(xt_all.at[pl.ds(0, far - 1)], rs_send.at[1])
@@ -600,8 +602,7 @@
 
     small_came(pw2, zs - 1, p_recv.at[2])
 
-    power_sibling().wait_send()
-    sent(pw1.at[pl.ds(0, planes - 1)], p_send.at[1])
+    sent(pw1.at[pl.ds(0, 2 * planes - 1)], p_send.at[0])
     sent(pw2.at[pl.ds(0, zs - 1)], p_send.at[2])
     power = jnp.sum(jnp.sum(pw2[...], axis=0), axis=0, keepdims=True)
     power = jnp.sum(power, axis=1, keepdims=True)
@@ -645,8 +646,7 @@
         pltpu.VMEM((SLOT, rows * TOK), BF16),
         *([pltpu.VMEM((2, quarter, PAD, TOK), BF16)] * 4),
         pltpu.VMEM((3, 8, TOK), F32),
-        pltpu.VMEM((8, TOK), F32),
-        pltpu.VMEM((planes, 8, TOK), F32),
+        pltpu.VMEM((2 * planes, 8, TOK), F32),
         pltpu.VMEM((zs, 8, TOK), F32),
         dma((7,)),
         dma((2,)), dma((2, 2, 2, quarter)),

time: 98 us -> 98.3 us (level)
  no operation moved by 1% of the time
where the time goes in v4:
time: 98.3 us; the launch traced here: 98.1 us
  Pallas kernels  96.7 us (98%)
  local copies, waits for them, and re-layouts  1.39 us (1%)
    pallas_call x1, Pallas kernels, shards(): pl.pallas_call(functools.partial(kernel, (depths, los, ys, zs)), out_shap...  96.7 us

profile of v4, /device:TPU:1, one launch (start us, length us, event | category | flops | bytes accessed | tf_op | source)
XLA Modules:
  0.0 98.1 jit_solution(11521475309394036374)
XLA Ops:
  0.0 96.7 %shard_map.73 = bf16[152,128]{1,0:T(8,128)(2,1)} custom-call(bf16[152,128]{1,0:T(8,128)(2,1)} %bitcast.4, bf16[152,128]{1,0:T(8,128)(2,1)} %bitcast.5, bf16[152,128]{1,0:T(8,128)(2,1)} %wq_hbm.1, bf16[152,128]{1,0:T(8,128)(2,1)} %wk_hbm.1, bf16[152,128]{1,0:T(8,128)(2,1)} %wv_hbm.1, bf16[152,128]{1,0:T(8,128)(2,1)} %wo_hbm.1, bf16[152]{0:T(256)(128)(2,1)} %gain_hbm.1), custom_call_target="tpu_custom_call" | custom-call | tf_op jit(solution)/shard_map/pallas_call | solution.py:661
  96.7 1.4 %copy.9 = bf16[128,152]{0,1:T(8,128)(2,1)} copy(bf16[128,152]{0,1:T(8,128)(2,1)} %bitcast.3) | data formatting | bytes 77824

commit v5 on v4

--- a/solution.py
+++ b/solution.py
@@ -137,36 +137,17 @@
     pl.semaphore_wait(barrier, len({by % zs for by in (1, -1, 2, -2)}) + planes)
 
     streams = (xt_all, og_all)
-
-    def tree(stream, side, leaf, k):
+    steps = (zs // 2, zs - 1 - zs // 2)
+
+    def ring(stream, side, step):
         sign = -1 if side else 1
-        slot = streams[stream].at[z_at(-2 * k * sign)]
-        to = z_device(sign if leaf else 2 * sign)
-        return remote(slot, slot, z_send.at[stream], z_recv.at[stream, side, leaf, k], to)
-
-    def tree_came(stream, side, leaf, k):
+        slot = streams[stream].at[z_at(-sign * step)]
+        return remote(slot, slot, z_send.at[stream], z_recv.at[stream, side, step], z_device(sign))
+
+    def ring_came(stream, side, step):
         sign = -1 if side else 1
-        slot = streams[stream].at[z_at(-(2 * k + (1 if leaf else 2)) * sign)]
-        remote(slot, slot, z_send.at[stream], z_recv.at[stream, side, leaf, k], sibling).wait_recv()
-
-    def tree_round(stream, k):
-        if k:
-            tree_came(stream, 0, 0, k - 1)
-        tree(stream, 0, 0, k).start()
-        if k:
-            tree(stream, 0, 1, k).start()
-            tree_came(stream, 1, 0, k - 1)
-        if k < quarter - 1:
-            tree(stream, 1, 0, k).start()
-        if not k:
-            tree(stream, 0, 1, k).start()
-        tree(stream, 1, 1, k).start()
-
-    def tree_end(stream):
-        tree_came(stream, 0, 0, quarter - 1)
-        for k in range(quarter):
-            tree_came(stream, 0, 1, k)
-            tree_came(stream, 1, 1, k)
+        slot = streams[stream].at[z_at(-sign * (step + 1))]
+        remote(slot, slot, z_send.at[stream], z_recv.at[stream, side, step], sibling).wait_recv()
 
     def column_device(up):
         return (d, (lo * ys + lax.rem(y + up % ys, ys)) * 2 + core, c)
@@ -243,35 +224,45 @@
     def sent(ref, sem):
         remote(ref, ref, sem, p_recv.at[0], sibling).wait_send()
 
-    tree_round(0, 0)
+    for side in range(2):
+        ring(0, side, 0).start()
+    fetches[1].wait()
+    og_all[c] = padded(og_ref)
+    for side in range(2):
+        ring(1, side, 0).start()
     fetches[3].wait()
     fetches[4].wait()
     wkv_all[lo, y, core] = jnp.concatenate([padded(wk_ref), padded(wv_ref)], axis=1)
     weight_first(0)
     weight_x_one(0, 0)
-    for i in (1, 5, 6):
-        fetches[i].wait()
+    fetches[5].wait()
+    fetches[6].wait()
     wqo_all[lo, y, core] = jnp.concatenate([padded(wq_ref), padded(wo_ref)], axis=1)
+    weight_first(1)
     og_own[...] = padded(og_ref).astype(F32)
-    og_all[c] = padded(og_ref)
-    for k in range(1, quarter):
-        tree_round(0, k)
-        if k == 1:
-            weight_near(0)
-        if k == 2:
-            weight_column(0)
-    if quarter < 2:
-        weight_near(0)
-    if quarter < 3:
-        weight_column(0)
-    weight_first(1)
-    tree_round(1, 0)
-    weight_crossed(0)
-    tree_end(0)
-    weight_near(1)
+    schedule = [
+        [lambda: weight_near(0)],
+        [lambda: weight_near(1)],
+        [lambda: weight_column(0)],
+        [lambda: weight_column(1)],
+        [lambda: weight_crossed(0)],
+        [],
+        [lambda: weight_crossed(1)],
+    ]
+
+    for step in range(1, steps[0]):
+        for stream in range(2):
+            for side in range(2):
+                ring_came(stream, side, step - 1)
+                if step < steps[side]:
+                    ring(stream, side, step).start()
+        last = step == steps[0] - 1
+        for events in schedule[step - 1 :] if last else schedule[step - 1 : step]:
+            for event in events:
+                event()
+
+    ring_came(0, 0, steps[0] - 1)
     weight_all(0)
-    if quarter > 1:
-        tree_round(1, 1)
 
     tails = jnp.zeros((16, TOK), F32)
     for j in range(zs):
@@ -347,24 +338,13 @@
     kv = (project(xt_all, wkv_all, slice(0, SLOT)) * scale_two).astype(BF16)
     kv_all[lo, y, core] = kv
     slot_start(0)
-    weight_column(1)
-    if quarter > 2:
-        tree_round(1, 2)
-    slot_out(0, 1)
-    slot_near(0, 0)
-    weight_crossed(1)
-    if quarter > 3:
-        tree_round(1, 3)
-    slot_near(0, 1)
+    ring_came(1, 0, steps[0] - 1)
     weight_all(1)
     queries = (project(xt_all, wqo_all, slice(0, WIDE)) * scale_wide).astype(BF16)
-    slot_far(0, 0)
-    tree_end(1)
     out_dir = project(og_all, wqo_all, slice(WIDE, SLOT)).astype(BF16)
     scaled_queries = (queries.astype(F32) * 0.125).astype(BF16)
     qd_all[lo, y, core] = jnp.concatenate([scaled_queries, out_dir], axis=1)
     slot_start(1)
-    slot_far(0, 1)
     low = lax.broadcasted_iota(jnp.int32, (TOK, WIDE), 1) < HDIM
 
     def stacked(a):
@@ -387,13 +367,18 @@
         kt_ref[parity] = jnp.transpose(keys)
         return jnp.max(scores.reshape(chips * TOK // 8, 8, SLOT), axis=0)
 
+    slot_out(0, 1)
+    slot_near(0, 0)
+    slot_out(1, 1)
+    slot_near(0, 1)
+    slot_far(0, 0)
+    slot_near(1, 0)
+    slot_far(0, 1)
     most = scores_of(core)
-    slot_out(1, 1)
-    slot_near(1, 0)
+    slot_near(1, 1)
+    slot_far(1, 0)
     slot_all(0)
     most = jnp.max(jnp.maximum(most, scores_of(other)), axis=0, keepdims=True)
-    slot_near(1, 1)
-    slot_far(1, 0)
 
     def tile_at(i):
         return i // (2 * ys), lax.rem(i // 2, ys), lax.rem(i, 2)
@@ -649,7 +634,7 @@
         pltpu.VMEM((2 * planes, 8, TOK), F32),
         pltpu.VMEM((zs, 8, TOK), F32),
         dma((7,)),
-        dma((2,)), dma((2, 2, 2, quarter)),
+        dma((2,)), dma((2, 2, 2 * quarter)),
         dma((2, 3)), dma((2, ys + 1)), dma((2,)),
         dma((2, 3)), dma((2, los, ys)), dma((2,)),
         dma, dma,

time: 98.3 us -> 95.7 us (0.974)
  Pallas kernels: 96.7 us -> 94 us
    pallas_call x1, Pallas kernels: 96.7 us -> 94 us  [shards(): pl.pallas_call(functools.partial(kernel, (depths, los, ys, zs)), out_shap...]
where the time goes in v5:
time: 95.7 us; the launch traced here: 95.4 us
  Pallas kernels  94 us (98%)
  local copies, waits for them, and re-layouts  1.39 us (1%)
    pallas_call x1, Pallas kernels, shards(): pl.pallas_call(functools.partial(kernel, (depths, los, ys, zs)), out_shap...  94 us

profile of v5, /device:TPU:1, one launch (start us, length us, event | category | flops | bytes accessed | tf_op | source)
XLA Modules:
  0.0 95.4 jit_solution(1504370354138715338)
XLA Ops:
  0.0 94.0 %shard_map.73 = bf16[152,128]{1,0:T(8,128)(2,1)} custom-call(bf16[152,128]{1,0:T(8,128)(2,1)} %bitcast.4, bf16[152,128]{1,0:T(8,128)(2,1)} %bitcast.5, bf16[152,128]{1,0:T(8,128)(2,1)} %wq_hbm.1, bf16[152,128]{1,0:T(8,128)(2,1)} %wk_hbm.1, bf16[152,128]{1,0:T(8,128)(2,1)} %wv_hbm.1, bf16[152,128]{1,0:T(8,128)(2,1)} %wo_hbm.1, bf16[152]{0:T(256)(128)(2,1)} %gain_hbm.1), custom_call_target="tpu_custom_call" | custom-call | tf_op jit(solution)/shard_map/pallas_call | solution.py:646
  94.0 1.4 %copy.9 = bf16[128,152]{0,1:T(8,128)(2,1)} copy(bf16[128,152]{0,1:T(8,128)(2,1)} %bitcast.3) | data formatting | bytes 77824

commit v6 on v5

--- a/solution.py
+++ b/solution.py
@@ -47,7 +47,7 @@
     xt_own, og_own, gain_own,
     s_ref, dp_ref, kt_ref, ds_ref, s2_ref, dp2_ref, p2_ref, ds2_ref,
     rs_leaf_tx, rs_hub_tx, rs_leaf, rs_hub,
-    pw_tx, pw1, pw2,
+    pw_tx, pw0, pw1, pw2,
     in_sem,
     z_send, z_recv,
     w_send, w_recv, wsib_recv,
@@ -95,21 +95,19 @@
     inputs = (lat_hbm, og_hbm, gain_hbm, wk_hbm, wv_hbm, wq_hbm, wo_hbm)
     staged = (lat_ref, og_ref, gain_ref, wk_ref, wv_ref, wq_ref, wo_ref)
     fetches = [pltpu.make_async_copy(a, b, in_sem.at[i]) for i, (a, b) in enumerate(zip(inputs, staged))]
-    for fetch in fetches:
-        fetch.start()
-
+    for i in (0, 2, 1, 3, 4, 5, 6):
+        fetches[i].start()
+
+    near_z = sorted({by % zs for by in (1, -1, 2, -2)})
+    near_y = sorted({by % ys for by in (1, -1)} - {0})
+    near_x = sorted({by % xs for by in (1, -1)})
     barrier = pltpu.get_barrier_semaphore()
-
-    def greet(device):
+    partners = [(d, r, lax.rem(c + by, zs)) for by in near_z]
+    partners += [plane_device(x * ys + lax.rem(y + by, ys)) for by in near_y]
+    partners += [plane_device(lax.rem(x + by, xs) * ys + y) for by in near_x]
+    partners += [sibling]
+    for device in partners:
         pl.semaphore_signal(barrier, inc=1, device_id=device, device_id_type=MESH)
-
-    for by in sorted({by % zs for by in (1, -1, 2, -2)}):
-        greet(z_device(by))
-    greet(sibling)
-
-    @pl.loop(1, planes)
-    def _(i):
-        greet(plane_device(lax.rem(here + i, planes)))
 
     fetches[0].wait()
     fetches[2].wait()
@@ -134,20 +132,47 @@
     xt_all[c] = sent.astype(BF16)
     xt_own[...] = xt
     gain_own[...] = gain_wide
-    pl.semaphore_wait(barrier, len({by % zs for by in (1, -1, 2, -2)}) + planes)
+    pl.semaphore_wait(barrier, len(partners))
 
     streams = (xt_all, og_all)
-    steps = (zs // 2, zs - 1 - zs // 2)
-
-    def ring(stream, side, step):
+
+    def edges(most):
+        a, found = 0, []
+        while a < most:
+            if a + 2 <= most and a < 4:
+                found += [(a, a + 2), (a, a + 1)]
+                a += 2
+            else:
+                found += [(a, a + 1)]
+                a += 1
+        return found
+
+    ways = (edges(zs // 2), edges(zs - 1 - zs // 2))
+    stops = sorted({a for way in ways for a, b in way})
+
+    def ring(stream, side, a, b):
         sign = -1 if side else 1
-        slot = streams[stream].at[z_at(-sign * step)]
-        return remote(slot, slot, z_send.at[stream], z_recv.at[stream, side, step], z_device(sign))
-
-    def ring_came(stream, side, step):
+        slot = streams[stream].at[z_at(-sign * a)]
+        return remote(slot, slot, z_send.at[stream], z_recv.at[stream, side, b - 1], z_device(sign * (b - a)))
+
+    def ring_came(stream, side, b):
         sign = -1 if side else 1
-        slot = streams[stream].at[z_at(-sign * (step + 1))]
-        remote(slot, slot, z_send.at[stream], z_recv.at[stream, side, step], sibling).wait_recv()
+        slot = streams[stream].at[z_at(-sign * b)]
+        remote(slot, slot, z_send.at[stream], z_recv.at[stream, side, b - 1], sibling).wait_recv()
+
+    def ring_round(stream, stop):
+        for side in range(2):
+            out = [edge for edge in ways[side] if edge[0] == stop]
+            if out and stop:
+                ring_came(stream, side, stop)
+            for edge in out:
+                ring(stream, side, *edge).start()
+
+    def ring_end(stream):
+        for side in range(2):
+            for a, b in ways[side]:
+                if b not in [start for start, end in ways[side]]:
+                    ring_came(stream, side, b)
 
     def column_device(up):
         return (d, (lo * ys + lax.rem(y + up % ys, ys)) * 2 + core, c)
@@ -224,12 +249,10 @@
     def sent(ref, sem):
         remote(ref, ref, sem, p_recv.at[0], sibling).wait_send()
 
-    for side in range(2):
-        ring(0, side, 0).start()
+    ring_round(0, 0)
     fetches[1].wait()
     og_all[c] = padded(og_ref)
-    for side in range(2):
-        ring(1, side, 0).start()
+    ring_round(1, 0)
     fetches[3].wait()
     fetches[4].wait()
     wkv_all[lo, y, core] = jnp.concatenate([padded(wk_ref), padded(wv_ref)], axis=1)
@@ -244,24 +267,24 @@
         [lambda: weight_near(0)],
         [lambda: weight_near(1)],
         [lambda: weight_column(0)],
-        [lambda: weight_column(1)],
-        [lambda: weight_crossed(0)],
-        [],
+        [lambda: weight_column(1), lambda: weight_crossed(0)],
         [lambda: weight_crossed(1)],
     ]
 
-    for step in range(1, steps[0]):
-        for stream in range(2):
-            for side in range(2):
-                ring_came(stream, side, step - 1)
-                if step < steps[side]:
-                    ring(stream, side, step).start()
-        last = step == steps[0] - 1
-        for events in schedule[step - 1 :] if last else schedule[step - 1 : step]:
+    for n, stop in enumerate(stops[1:]):
+        ring_round(0, stop)
+        ring_round(1, stop)
+        last = n == len(stops) - 2
+        for events in schedule[n:] if last else schedule[n : n + 1]:
             for event in events:
                 event()
 
-    ring_came(0, 0, steps[0] - 1)
+    if len(stops) == 1:
+        for events in schedule:
+            for event in events:
+                event()
+
+    ring_end(0)
     weight_all(0)
 
     tails = jnp.zeros((16, TOK), F32)
@@ -338,7 +361,7 @@
     kv = (project(xt_all, wkv_all, slice(0, SLOT)) * scale_two).astype(BF16)
     kv_all[lo, y, core] = kv
     slot_start(0)
-    ring_came(1, 0, steps[0] - 1)
+    ring_end(1)
     weight_all(1)
     queries = (project(xt_all, wqo_all, slice(0, WIDE)) * scale_wide).astype(BF16)
     out_dir = project(og_all, wqo_all, slice(WIDE, SLOT)).astype(BF16)
@@ -405,20 +428,24 @@
 
     def small_came(ref, count, sem):
         some = ref.at[pl.ds(0, count)]
-        remote(some, some, p_send.at[1], sem, sibling).wait_recv()
+        remote(some, some, p_send.at[0], sem, sibling).wait_recv()
 
     st_all[r] = jnp.concatenate([most + jnp.log(totals), delta, jnp.zeros((6, SLOT), F32)], axis=0)
 
-    @pl.loop(1, rows)
-    def _(i):
-        stat_copy(i).start()
-
-    def score_grad_body(i, nothing):
+    def score_grad(i):
         at = tile_at(i)
         ds_ref[at] = (s_ref[at] * (dp_ref[at] - delta)).astype(BF16)
+
+    def score_grad_body(i, nothing):
+        stat_copy(lax.rem(rows // 2 + i, rows)).start()
+        score_grad(i)
         return nothing
 
-    lax.fori_loop(0, rows, score_grad_body, 0, unroll=2)
+    stat_copy(rows // 2).start()
+    lax.fori_loop(1, rows // 2, score_grad_body, 0)
+    lax.fori_loop(rows // 2 + 1, rows, score_grad_body, 0)
+    score_grad(0)
+    score_grad(rows // 2)
     query_grad = jnp.zeros((WIDE, SLOT), F32)
     for parity in range(2):
         query_grad = query_grad + dot_nn(kt_ref[parity], slots_of(ds_ref, parity, slice(0, SLOT)))
@@ -552,44 +579,41 @@
     raw = og_own[...] + scale_row * (scaled - normalized * inner)
     power = jnp.sum((raw * raw).reshape(PAD // 8, 8, TOK), axis=0)
 
-    def power_sibling():
-        return remote(pw_tx.at[0], pw1.at[here * 2 + core], p_send.at[0], p_recv.at[0], sibling)
-
-    def power_plane(i, of_core):
-        to = lax.rem(here + i, planes)
-        to_d, to_r, to_c = plane_device(to)
-        to_r = to_r - core + of_core
-        return remote(pw_tx.at[0], pw1.at[here * 2 + core], p_send.at[0], p_recv.at[0], (to_d, to_r, to_c))
-
-    def power_col(i):
-        return remote(pw_tx.at[2], pw2.at[c], p_send.at[2], p_recv.at[2], (d, r, lax.rem(c + i, zs)))
-
-    pw_tx[0] = power
-    pw1[here * 2 + core] = power
-    power_sibling().start()
-
-    @pl.loop(1, planes)
-    def _(i):
-        power_plane(i, 0).start()
-        power_plane(i, 1).start()
-
-    small_came(pw1, 2 * planes - 1, p_recv.at[0])
-
-    sent(xt_all.at[pl.ds(0, far)], rs_send.at[0])
-    sent(xt_all.at[pl.ds(0, far - 1)], rs_send.at[1])
-    power = jnp.sum(pw1[...], axis=0)
-    pw_tx[2] = power
-    pw2[c] = power
-
-    @pl.loop(1, zs)
-    def _(i):
-        power_col(i).start()
-
-    small_came(pw2, zs - 1, p_recv.at[2])
-
-    sent(pw1.at[pl.ds(0, 2 * planes - 1)], p_send.at[0])
-    sent(pw2.at[pl.ds(0, zs - 1)], p_send.at[2])
-    power = jnp.sum(jnp.sum(pw2[...], axis=0), axis=0, keepdims=True)
+    def far_first(n):
+        return sorted(range(1, n), key=lambda i: -min(i, n - i))
+
+    def power_stage(stage, landing, me, n, device):
+        copies = [
+            remote(pw_tx.at[stage], landing.at[me], p_send.at[stage], p_recv.at[stage], device(i)) for i in far_first(n)
+        ]
+        for copy in copies:
+            copy.start()
+        return copies
+
+    def power_column(i):
+        at = lax.rem(y * 2 + core + i, 2 * ys)
+        return (d, lo * ys * 2 + at, c)
+
+    def power_x(i):
+        return plane_device(lax.rem(x + i, xs) * ys + y)
+
+    stages = (
+        (pw0, y * 2 + core, 2 * ys, power_column),
+        (pw1, x, xs, power_x),
+        (pw2, c, zs, z_device),
+    )
+    for stage, (landing, me, n, device) in enumerate(stages):
+        pw_tx[stage] = power
+        landing[me] = power
+        power_stage(stage, landing, me, n, device)
+        if stage == 0:
+            sent(xt_all.at[pl.ds(0, far)], rs_send.at[0])
+            sent(xt_all.at[pl.ds(0, far - 1)], rs_send.at[1])
+        small_came(landing, n - 1, p_recv.at[stage])
+        sent(landing.at[pl.ds(0, n - 1)], p_send.at[stage])
+        power = jnp.sum(landing[...], axis=0)
+
+    power = jnp.sum(power, axis=0, keepdims=True)
     power = jnp.sum(power, axis=1, keepdims=True)
     cells = depths * seq * zs * FEAT
     final = raw * lax.rsqrt(power * (1.0 / cells) + epsilon)
@@ -631,7 +655,8 @@
         pltpu.VMEM((SLOT, rows * TOK), BF16),
         *([pltpu.VMEM((2, quarter, PAD, TOK), BF16)] * 4),
         pltpu.VMEM((3, 8, TOK), F32),
-        pltpu.VMEM((2 * planes, 8, TOK), F32),
+        pltpu.VMEM((2 * ys, 8, TOK), F32),
+        pltpu.VMEM((depths * los, 8, TOK), F32),
         pltpu.VMEM((zs, 8, TOK), F32),
         dma((7,)),
         dma((2,)), dma((2, 2, 2 * quarter)),

time: 95.7 us -> 93.8 us (0.980)
  Pallas kernels: 94 us -> 92 us
    pallas_call x1, Pallas kernels: 94 us -> 92 us  [shards(): pl.pallas_call(functools.partial(kernel, (depths, los, ys, zs)), out_shap...]
where the time goes in v6:
time: 93.8 us; the launch traced here: 93.4 us
  Pallas kernels  92 us (98%)
  local copies, waits for them, and re-layouts  1.39 us (1%)
    pallas_call x1, Pallas kernels, shards(): pl.pallas_call(functools.partial(kernel, (depths, los, ys, zs)), out_shap...  92 us

profile of v6, /device:TPU:1, one launch (start us, length us, event | category | flops | bytes accessed | tf_op | source)
XLA Modules:
  0.0 93.4 jit_solution(8047531962841159139)
XLA Ops:
  0.0 92.0 %shard_map.73 = bf16[152,128]{1,0:T(8,128)(2,1)} custom-call(bf16[152,128]{1,0:T(8,128)(2,1)} %bitcast.4, bf16[152,128]{1,0:T(8,128)(2,1)} %bitcast.5, bf16[152,128]{1,0:T(8,128)(2,1)} %wq_hbm.1, bf16[152,128]{1,0:T(8,128)(2,1)} %wk_hbm.1, bf16[152,128]{1,0:T(8,128)(2,1)} %wv_hbm.1, bf16[152,128]{1,0:T(8,128)(2,1)} %wo_hbm.1, bf16[152]{0:T(256)(128)(2,1)} %gain_hbm.1), custom_call_target="tpu_custom_call" | custom-call | tf_op jit(solution)/shard_map/pallas_call | solution.py:671
  92.0 1.4 %copy.9 = bf16[128,152]{0,1:T(8,128)(2,1)} copy(bf16[128,152]{0,1:T(8,128)(2,1)} %bitcast.3) | data formatting | bytes 77824

commit v7 on v6

--- a/solution.py
+++ b/solution.py
@@ -43,7 +43,7 @@
     lat_hbm, og_hbm, wq_hbm, wk_hbm, wv_hbm, wo_hbm, gain_hbm,
     out_ref,
     lat_ref, og_ref, wq_ref, wk_ref, wv_ref, wo_ref, gain_ref,
-    xt_all, og_all, wkv_all, wqo_all, kv_all, qd_all, st_all,
+    xt_all, og_all, xn_all, on_all, wkv_all, wqo_all, kv_all, qd_all, st_all,
     xt_own, og_own, gain_own,
     s_ref, dp_ref, kt_ref, ds_ref, s2_ref, dp2_ref, p2_ref, ds2_ref,
     rs_leaf_tx, rs_hub_tx, rs_leaf, rs_hub,
@@ -139,12 +139,8 @@
     def edges(most):
         a, found = 0, []
         while a < most:
-            if a + 2 <= most and a < 4:
-                found += [(a, a + 2), (a, a + 1)]
-                a += 2
-            else:
-                found += [(a, a + 1)]
-                a += 1
+            found += [(a, a + 1)]
+            a += 1
         return found
 
     ways = (edges(zs // 2), edges(zs - 1 - zs // 2))
@@ -160,19 +156,30 @@
         slot = streams[stream].at[z_at(-sign * b)]
         remote(slot, slot, z_send.at[stream], z_recv.at[stream, side, b - 1], sibling).wait_recv()
 
+    turn = eye(TOK, TOK)
+
+    def turn_block(stream, by):
+        j = z_at(by)
+        (xn_all, on_all)[stream][j] = dot_nt(turn, streams[stream][j]).astype(BF16)
+
     def ring_round(stream, stop):
-        for side in range(2):
-            out = [edge for edge in ways[side] if edge[0] == stop]
-            if out and stop:
+        sides = [side for side in range(2) if (stop, stop + 1) in ways[side]]
+        for side in sides:
+            if stop:
                 ring_came(stream, side, stop)
-            for edge in out:
-                ring(stream, side, *edge).start()
+            ring(stream, side, stop, stop + 1).start()
+
+    def ring_turn(stream, stop):
+        turn_block(stream, -stop)
+        if stop and (stop, stop + 1) in ways[1]:
+            turn_block(stream, stop)
 
     def ring_end(stream):
         for side in range(2):
-            for a, b in ways[side]:
-                if b not in [start for start, end in ways[side]]:
-                    ring_came(stream, side, b)
+            stop = len(ways[side])
+            if stop:
+                ring_came(stream, side, stop)
+                turn_block(stream, stop if side else -stop)
 
     def column_device(up):
         return (d, (lo * ys + lax.rem(y + up % ys, ys)) * 2 + core, c)
@@ -263,17 +270,23 @@
     wqo_all[lo, y, core] = jnp.concatenate([padded(wq_ref), padded(wo_ref)], axis=1)
     weight_first(1)
     og_own[...] = padded(og_ref).astype(F32)
+    ring_turn(0, 0)
+    ring_turn(1, 0)
     schedule = [
         [lambda: weight_near(0)],
         [lambda: weight_near(1)],
         [lambda: weight_column(0)],
-        [lambda: weight_column(1), lambda: weight_crossed(0)],
+        [lambda: weight_column(1)],
+        [lambda: weight_crossed(0)],
+        [],
         [lambda: weight_crossed(1)],
     ]
 
     for n, stop in enumerate(stops[1:]):
         ring_round(0, stop)
         ring_round(1, stop)
+        ring_turn(0, stop)
+        ring_turn(1, stop)
         last = n == len(stops) - 2
         for events in schedule[n:] if last else schedule[n : n + 1]:
             for event in events:
@@ -298,13 +311,10 @@
 
     def project(source, weight, lanes):
         total = None
-        for of_lo in range(los):
-            for of_y in range(0, ys, pair):
-                first = (of_lo * ys + of_y) * 2
-                a = source[first : first + 2 * pair].reshape(2 * pair * PAD, TOK)
-                b = weight[of_lo, of_y : of_y + pair, :, :, lanes]
-                term = dot_tn(a, b.reshape(2 * pair * PAD, b.shape[-1]))
-                total = term if total is None else total + term
+        for j in range(zs):
+            at = (j // (2 * ys), j // 2 % ys, j % 2, slice(None), lanes)
+            term = dot_nn(source[j], weight[at])
+            total = term if total is None else total + term
         return total
 
     gathered = (kv_all, qd_all)
@@ -358,13 +368,13 @@
         slot = gathered[array].at[:, :, other]
         remote(slot, slot, a_send.at[array, 2], asib_recv.at[array], sibling).wait_recv()
 
-    kv = (project(xt_all, wkv_all, slice(0, SLOT)) * scale_two).astype(BF16)
+    kv = (project(xn_all, wkv_all, slice(0, SLOT)) * scale_two).astype(BF16)
     kv_all[lo, y, core] = kv
     slot_start(0)
     ring_end(1)
     weight_all(1)
-    queries = (project(xt_all, wqo_all, slice(0, WIDE)) * scale_wide).astype(BF16)
-    out_dir = project(og_all, wqo_all, slice(WIDE, SLOT)).astype(BF16)
+    queries = (project(xn_all, wqo_all, slice(0, WIDE)) * scale_wide).astype(BF16)
+    out_dir = project(on_all, wqo_all, slice(WIDE, SLOT)).astype(BF16)
     scaled_queries = (queries.astype(F32) * 0.125).astype(BF16)
     qd_all[lo, y, core] = jnp.concatenate([scaled_queries, out_dir], axis=1)
     slot_start(1)
@@ -637,6 +647,8 @@
         pltpu.VMEM((FEAT,), BF16),
         pltpu.VMEM((zs, PAD, TOK), BF16),
         pltpu.VMEM((zs, PAD, TOK), BF16),
+        pltpu.VMEM((zs, TOK, PAD), BF16),
+        pltpu.VMEM((zs, TOK, PAD), BF16),
         pltpu.VMEM((los, ys, 2, PAD, SLOT), BF16),
         pltpu.VMEM((los, ys, 2, PAD, SLOT), BF16),
         pltpu.VMEM((los, ys, 2, TOK, SLOT), BF16),

time: 93.8 us -> 96.7 us (1.031)
  Pallas kernels: 92 us -> 94.6 us
    pallas_call x1, Pallas kernels: 92 us -> 94.6 us  [shards(): pl.pallas_call(functools.partial(kernel, (depths, los, ys, zs)), out_shap...]
where the time goes in v7:
time: 96.7 us; the launch traced here: 96 us
  Pallas kernels  94.6 us (98%)
  local copies, waits for them, and re-layouts  1.39 us (1%)
    pallas_call x1, Pallas kernels, shards(): pl.pallas_call(functools.partial(kernel, (depths, los, ys, zs)), out_shap...  94.6 us

profile of v7, /device:TPU:1, one launch (start us, length us, event | category | flops | bytes accessed | tf_op | source)
XLA Modules:
  0.0 96.0 jit_solution(6912609846325234008)
XLA Ops:
  0.0 94.6 %shard_map.73 = bf16[152,128]{1,0:T(8,128)(2,1)} custom-call(bf16[152,128]{1,0:T(8,128)(2,1)} %bitcast.4, bf16[152,128]{1,0:T(8,128)(2,1)} %bitcast.5, bf16[152,128]{1,0:T(8,128)(2,1)} %wq_hbm.1, bf16[152,128]{1,0:T(8,128)(2,1)} %wk_hbm.1, bf16[152,128]{1,0:T(8,128)(2,1)} %wv_hbm.1, bf16[152,128]{1,0:T(8,128)(2,1)} %wo_hbm.1, bf16[152]{0:T(256)(128)(2,1)} %gain_hbm.1), custom_call_target="tpu_custom_call" | custom-call | tf_op jit(solution)/shard_map/pallas_call | solution.py:683
  94.6 1.4 %copy.9 = bf16[128,152]{0,1:T(8,128)(2,1)} copy(bf16[128,152]{0,1:T(8,128)(2,1)} %bitcast.3) | data formatting | bytes 77824

commit v8 on v6

--- a/solution.py
+++ b/solution.py
@@ -267,8 +267,7 @@
         [lambda: weight_near(0)],
         [lambda: weight_near(1)],
         [lambda: weight_column(0)],
-        [lambda: weight_column(1), lambda: weight_crossed(0)],
-        [lambda: weight_crossed(1)],
+        [lambda: weight_crossed(0), lambda: weight_column(1)],
     ]
 
     for n, stop in enumerate(stops[1:]):
@@ -361,13 +360,19 @@
     kv = (project(xt_all, wkv_all, slice(0, SLOT)) * scale_two).astype(BF16)
     kv_all[lo, y, core] = kv
     slot_start(0)
+    slot_out(0, 1)
+    slot_near(0, 0)
+    weight_crossed(1)
     ring_end(1)
     weight_all(1)
     queries = (project(xt_all, wqo_all, slice(0, WIDE)) * scale_wide).astype(BF16)
+    slot_near(0, 1)
+    slot_far(0, 0)
     out_dir = project(og_all, wqo_all, slice(WIDE, SLOT)).astype(BF16)
     scaled_queries = (queries.astype(F32) * 0.125).astype(BF16)
     qd_all[lo, y, core] = jnp.concatenate([scaled_queries, out_dir], axis=1)
     slot_start(1)
+    slot_far(0, 1)
     low = lax.broadcasted_iota(jnp.int32, (TOK, WIDE), 1) < HDIM
 
     def stacked(a):
@@ -390,18 +395,13 @@
         kt_ref[parity] = jnp.transpose(keys)
         return jnp.max(scores.reshape(chips * TOK // 8, 8, SLOT), axis=0)
 
-    slot_out(0, 1)
-    slot_near(0, 0)
+    most = scores_of(core)
     slot_out(1, 1)
-    slot_near(0, 1)
-    slot_far(0, 0)
     slot_near(1, 0)
-    slot_far(0, 1)
-    most = scores_of(core)
+    slot_all(0)
+    most = jnp.max(jnp.maximum(most, scores_of(other)), axis=0, keepdims=True)
     slot_near(1, 1)
     slot_far(1, 0)
-    slot_all(0)
-    most = jnp.max(jnp.maximum(most, scores_of(other)), axis=0, keepdims=True)
 
     def tile_at(i):
         return i // (2 * ys), lax.rem(i // 2, ys), lax.rem(i, 2)
@@ -579,16 +579,12 @@
     raw = og_own[...] + scale_row * (scaled - normalized * inner)
     power = jnp.sum((raw * raw).reshape(PAD // 8, 8, TOK), axis=0)
 
-    def far_first(n):
-        return sorted(range(1, n), key=lambda i: -min(i, n - i))
-
     def power_stage(stage, landing, me, n, device):
-        copies = [
-            remote(pw_tx.at[stage], landing.at[me], p_send.at[stage], p_recv.at[stage], device(i)) for i in far_first(n)
-        ]
-        for copy in copies:
-            copy.start()
-        return copies
+        @pl.loop(0, n - 1)
+        def _(m):
+            k = (m + 1) // 2
+            i = n // 2 + jnp.where(lax.rem(m, 2) == 0, k, -k)
+            remote(pw_tx.at[stage], landing.at[me], p_send.at[stage], p_recv.at[stage], device(i)).start()
 
     def power_column(i):
         at = lax.rem(y * 2 + core + i, 2 * ys)
@@ -600,7 +596,7 @@
     stages = (
         (pw0, y * 2 + core, 2 * ys, power_column),
         (pw1, x, xs, power_x),
-        (pw2, c, zs, z_device),
+        (pw2, c, zs, lambda i: (d, r, lax.rem(c + i, zs))),
     )
     for stage, (landing, me, n, device) in enumerate(stages):
         pw_tx[stage] = power

time: 93.8 us -> 97.1 us (1.035)
  Pallas kernels: 92 us -> 95.4 us
    pallas_call x1, Pallas kernels: 92 us -> 95.4 us  [shards(): pl.pallas_call(functools.partial(kernel, (depths, los, ys, zs)), out_shap...]
where the time goes in v8:
time: 97.1 us; the launch traced here: 96.8 us
  Pallas kernels  95.4 us (98%)
  local copies, waits for them, and re-layouts  1.39 us (1%)
    pallas_call x1, Pallas kernels, shards(): pl.pallas_call(functools.partial(kernel, (depths, los, ys, zs)), out_shap...  95.4 us

profile of v8, /device:TPU:1, one launch (start us, length us, event | category | flops | bytes accessed | tf_op | source)
XLA Modules:
  0.0 96.8 jit_solution(707205299734273967)
XLA Ops:
  0.0 95.4 %shard_map.73 = bf16[152,128]{1,0:T(8,128)(2,1)} custom-call(bf16[152,128]{1,0:T(8,128)(2,1)} %bitcast.4, bf16[152,128]{1,0:T(8,128)(2,1)} %bitcast.5, bf16[152,128]{1,0:T(8,128)(2,1)} %wq_hbm.1, bf16[152,128]{1,0:T(8,128)(2,1)} %wk_hbm.1, bf16[152,128]{1,0:T(8,128)(2,1)} %wv_hbm.1, bf16[152,128]{1,0:T(8,128)(2,1)} %wo_hbm.1, bf16[152]{0:T(256)(128)(2,1)} %gain_hbm.1), custom_call_target="tpu_custom_call" | custom-call | tf_op jit(solution)/shard_map/pallas_call | solution.py:667
  95.4 1.4 %copy.9 = bf16[128,152]{0,1:T(8,128)(2,1)} copy(bf16[128,152]{0,1:T(8,128)(2,1)} %bitcast.3) | data formatting | bytes 77824
